TPU v7x, 128 devices: a whole 4x4x4 slice. The times are simulated.
128 devices in a mesh: flow: 32 (over x, y, core), mech: 4 (over z).
Axes of the slice: x: 4, y: 4, z: 4, core: 2. Of those that a mesh axis runs over, the one named last changes fastest.
Arguments:
- source: float32 [2048, 128], P('flow'), may hold values from -6 to 6
- aperture_rest: float32 [2048, 128], P('flow'), may hold values from 0.5 to 2
- storage: float32 [2048, 128], P('flow'), may hold values from 0.5 to 2
- geometry: float32 [2048, 128], P('flow'), may hold values from 0.2 to 1
- tiles: float32 [2048, 128, 128], P('flow'), as said below
- near: bfloat16 [512, 512, 512], P('flow', None, 'mech'), may hold values from -0.25 to 0.25
- basis_in: float32 [262144, 64], P('flow'), may hold values from -0.01171875 to 0.01171875
- core: float32 [64, 64], replicated, may hold values from -0.75 to 0.75
- basis_out: float32 [262144, 64], P('flow'), may hold values from -0.75 to 0.75
Outputs:
- pressure: float32 [2048, 128], P('flow')
- aperture: float32 [2048, 128], P('flow')
Inputs may be any that keep to these rules, and one draw needn't show every extreme that they name: `tiles`: each tile is symmetric with its eigenvalues between 1 and 4.
All inputs are finite; a program needn't handle non-finite values.
Results may differ from a plain program's by a relative error of at most 0.00033.
Values sent between devices are 32-bit elements; how exact they have to be, the bound alone decides.
A program may use at most 64 MiB of HBM per device.

v0:
```python
import jax
import jax.numpy as jnp
from jax import lax
from jax.sharding import PartitionSpec as P

CG = 5


def extended(cells, sides, width):
    for axis, dim in sides:
        count = lax.axis_size(axis)
        ends = count - 1
        head = lax.slice_in_dim(cells, 0, width, axis=dim)
        tail = lax.slice_in_dim(cells, cells.shape[dim] - width, cells.shape[dim], axis=dim)
        cells = jnp.concatenate(
            [
                lax.ppermute(tail, axis, [(i, (i + 1) % count) for i in range(ends)]),
                cells,
                lax.ppermute(head, axis, [((i + 1) % count, i) for i in range(ends)]),
            ],
            axis=dim,
        )
    return cells


def exchange_faces(v):
    return extended(v, (("flow", 0),), 1)


def operate(v, tiles, scale, storage, cond_all):
    padded = exchange_faces(v)
    local = jnp.einsum("bij,bj->bi", tiles, scale * v, precision=lax.Precision.HIGHEST) * scale
    cond = cond_all[1:]
    cprv = cond_all[:-1]
    return storage * v + local + (cond + cprv) * v - cond * padded[2:] - cprv * padded[:-2]


def squares(residual):
    return lax.psum(jnp.sum(residual * residual), "flow")


def curving(direction, image):
    return lax.psum(jnp.sum(direction * image), "flow")


def solve_flow(source, tiles, scale, storage, cond_all):
    pressure = jnp.zeros_like(source)
    residual = source
    direction = source
    norm_now = squares(residual)
    for step in range(CG):
        image = operate(direction, tiles, scale, storage, cond_all)
        alpha = norm_now / curving(direction, image)
        pressure = pressure + alpha * direction
        residual = residual - alpha * image
        norm_next = squares(residual)
        direction = residual + norm_next / norm_now * direction
        norm_now = norm_next
    return pressure


def body(source, aperture_rest, storage, geometry, tiles, near, basis_in, core, basis_out):
    blocks, width = source.shape
    groups = lax.axis_size("mech")
    owner = lax.axis_index("mech")
    clusters = near.shape[0]
    span = near.shape[2]
    aperture = aperture_rest
    stacked = jnp.stack([aperture, geometry])
    padded = extended(stacked, (("flow", 1),), 1)
    ap_pad = padded[0]
    geo_pad = padded[1]
    cond_all = geo_pad[:-1] * (ap_pad[:-1] ** 3 + ap_pad[1:] ** 3) * 0.5
    scale = aperture**1.5
    pressure = solve_flow(source, tiles, scale, storage, cond_all)
    packed = pressure.astype(jnp.bfloat16).reshape(clusters, span * groups)
    piece = lax.dynamic_slice_in_dim(packed, owner * span, span, 1)
    partial_value = jnp.einsum(
        "cij,cj->ci", near, piece, preferred_element_type=jnp.float32
    ).reshape(blocks, width)
    coeffs = lax.psum(
        jnp.dot(pressure.reshape(-1), basis_in, precision=lax.Precision.HIGHEST), "flow"
    )
    mixed = jnp.dot(core, coeffs, precision=lax.Precision.HIGHEST)
    near_disp = lax.psum(partial_value, "mech")
    far_disp = jnp.dot(basis_out, mixed, precision=lax.Precision.HIGHEST).reshape(blocks, width)
    aperture = aperture_rest * (1.0 + 0.5 * jnp.tanh(near_disp + far_disp))
    return (pressure, aperture)


def solution(mesh):
    placed = (
        P("flow", None),
        P("flow", None),
        P("flow", None),
        P("flow", None),
        P("flow", None, None),
        P("flow", None, "mech"),
        P("flow", None),
        P(),
        P("flow", None),
    )
    return jax.shard_map(
        body,
        mesh=mesh,
        in_specs=placed,
        out_specs=(P("flow", None), P("flow", None)),
        check_vma=False,
    )
```

profile of v0, /device:TPU:1, one launch (start us, length us, event | category | flops | bytes accessed | tf_op | source)
XLA Modules:
  0.0 757.8 jit_solution(2552151746603958167)
XLA Ops:
  1.6 4.6 collective-permute-start
  10.7 3.6 collective-permute-start.3
  15.2 8.3 %fusion.44 = f32[64,1,128]{2,1,0:T(1,128)S(1)} fusion(f32[64,128,1]{1,2,0:T(1,128)S(1)} %bitcast.87, f32[64,128,128]{2,1,0:T(8,128)} %param.13), kind=kOutput, calls=%fused_computation.84 | convolution fusion | flops 12582912 | bytes 4259840 | tf_op jit(solution)/shard_map/bij,bj->bi/dot_general | solution.py:32
  24.3 62.2 %all-reduce = (f32[]{:T(128)}, f32[]{:T(128)}) all-reduce(f32[]{:T(128)} %get-tuple-element.3, f32[]{:T(128)} %get-tuple-element.2), channel_id=1, replica_groups=mesh['flow'=32,'mech'=4] {'flow'}, use_global_device_ids=true, to_apply=%region_1.0 | all-reduce | flops 2 | bytes 16 | tf_op jit(solution)/shard_map/psum | solution.py:39
  88.4 67.2 %psum.86 = f32[]{:T(128)} all-reduce(f32[]{:T(128)} %multiply_reduce_fusion.6), channel_id=1, replica_groups=mesh['flow'=32,'mech'=4] {'flow'}, use_global_device_ids=true, to_apply=%region_5.0 | all-reduce | flops 1 | bytes 8 | tf_op jit(solution)/shard_map/psum | solution.py:39
  159.6 3.0 collective-permute-start.5
  162.6 8.3 %fusion.45 = f32[64,1,128]{2,1,0:T(1,128)S(1)} fusion(f32[64,128,1]{1,2,0:T(1,128)S(1)} %bitcast.81, f32[64,128,128]{2,1,0:T(8,128)} %param.13), kind=kOutput, calls=%fused_computation.85 | convolution fusion | flops 12582912 | bytes 4259840 | tf_op jit(solution)/shard_map/bij,bj->bi/dot_general | solution.py:32
  171.6 62.0 %psum.87 = f32[]{:T(128)} all-reduce(f32[]{:T(128)} %get-tuple-element.22), channel_id=1, replica_groups=mesh['flow'=32,'mech'=4] {'flow'}, use_global_device_ids=true, to_apply=%region_7.0 | all-reduce | flops 1 | bytes 8 | tf_op jit(solution)/shard_map/psum | solution.py:43
  235.6 64.4 %psum.88 = f32[]{:T(128)} all-reduce(f32[]{:T(128)} %get-tuple-element.20), channel_id=1, replica_groups=mesh['flow'=32,'mech'=4] {'flow'}, use_global_device_ids=true, to_apply=%region_9.0 | all-reduce | flops 1 | bytes 8 | tf_op jit(solution)/shard_map/psum | solution.py:39
  303.9 3.0 collective-permute-start.7
  306.9 8.3 %fusion.46 = f32[64,1,128]{2,1,0:T(1,128)S(1)} fusion(f32[64,128,1]{1,2,0:T(1,128)S(1)} %bitcast.82, f32[64,128,128]{2,1,0:T(8,128)} %param.13), kind=kOutput, calls=%fused_computation.86 | convolution fusion | flops 12582912 | bytes 4259840 | tf_op jit(solution)/shard_map/bij,bj->bi/dot_general | solution.py:32
  315.9 62.0 %psum.89 = f32[]{:T(128)} all-reduce(f32[]{:T(128)} %get-tuple-element.16), channel_id=1, replica_groups=mesh['flow'=32,'mech'=4] {'flow'}, use_global_device_ids=true, to_apply=%region_11.0 | all-reduce | flops 1 | bytes 8 | tf_op jit(solution)/shard_map/psum | solution.py:43
  379.9 64.4 %psum.90 = f32[]{:T(128)} all-reduce(f32[]{:T(128)} %get-tuple-element.14), channel_id=1, replica_groups=mesh['flow'=32,'mech'=4] {'flow'}, use_global_device_ids=true, to_apply=%region_13.0 | all-reduce | flops 1 | bytes 8 | tf_op jit(solution)/shard_map/psum | solution.py:39
  448.2 3.0 collective-permute-start.9
  451.3 8.3 %fusion.47 = f32[64,1,128]{2,1,0:T(1,128)S(1)} fusion(f32[64,128,1]{1,2,0:T(1,128)S(1)} %bitcast.83, f32[64,128,128]{2,1,0:T(8,128)} %param.13), kind=kOutput, calls=%fused_computation.87 | convolution fusion | flops 12582912 | bytes 4259840 | tf_op jit(solution)/shard_map/bij,bj->bi/dot_general | solution.py:32
  460.2 62.2 %psum.91 = f32[]{:T(128)} all-reduce(f32[]{:T(128)} %get-tuple-element.10), channel_id=1, replica_groups=mesh['flow'=32,'mech'=4] {'flow'}, use_global_device_ids=true, to_apply=%region_15.0 | all-reduce | flops 1 | bytes 8 | tf_op jit(solution)/shard_map/psum | solution.py:43
  524.4 64.4 %psum.92 = f32[]{:T(128)} all-reduce(f32[]{:T(128)} %multiply_reduce_fusion), channel_id=1, replica_groups=mesh['flow'=32,'mech'=4] {'flow'}, use_global_device_ids=true, to_apply=%region_17.0 | all-reduce | flops 1 | bytes 8 | tf_op jit(solution)/shard_map/psum | solution.py:39
  592.7 3.0 collective-permute-start.11
  595.8 8.3 %fusion.48 = f32[64,1,128]{2,1,0:T(1,128)S(1)} fusion(f32[64,128,1]{1,2,0:T(1,128)S(1)} %bitcast.89, f32[64,128,128]{2,1,0:T(8,128)} %param.13), kind=kOutput, calls=%fused_computation.88 | convolution fusion | flops 12582912 | bytes 4259840 | tf_op jit(solution)/shard_map/bij,bj->bi/dot_general | solution.py:32
  604.8 62.0 %psum.93 = f32[]{:T(128)} all-reduce(f32[]{:T(128)} %fusion.7), channel_id=1, replica_groups=mesh['flow'=32,'mech'=4] {'flow'}, use_global_device_ids=true, to_apply=%region_19.0 | all-reduce | flops 1 | bytes 8 | tf_op jit(solution)/shard_map/psum | solution.py:43
  668.9 14.6 %psum.94 = f32[64,128]{1,0:T(8,128)S(1)} all-reduce(f32[64,128]{1,0:T(8,128)S(1)} %reshape.20), channel_id=1, replica_groups=mesh['flow'=32,'mech'=4] {'mech'}, use_global_device_ids=true, to_apply=%region_20.0 | all-reduce | flops 8192 | bytes 65536 | tf_op jit(solution)/shard_map/psum | solution.py:85
  683.5 3.3 convolution_bitcast_fusion.1
  686.8 67.5 %psum.95 = f32[64]{0:T(128)S(1)} all-reduce(f32[64]{0:T(128)S(1)} %convolution_bitcast_fusion.1), channel_id=1, replica_groups=mesh['flow'=32,'mech'=4] {'flow'}, use_global_device_ids=true, to_apply=%region_21.0 | all-reduce | flops 64 | bytes 512 | tf_op jit(solution)/shard_map/psum | solution.py:81
  754.5 2.7 fusion.49
  (62 shorter events, 23.9 us)
Async XLA Ops:
  0.6 667.6 %copy-start = (bf16[16,512,128]{2,1,0:T(8,128)(2,1)S(1)}, bf16[16,512,128]{2,1,0:T(8,128)(2,1)}, u32[]{:S(2)}) copy-start(bf16[16,512,128]{2,1,0:T(8,128)(2,1)} %param.14) | copy-start | bytes 6291460
  0.6 22.8 %copy-start.1 = (f32[64,128]{1,0:T(8,128)S(1)}, f32[64,128]{1,0:T(8,128)}, u32[]{:S(2)}) copy-start(f32[64,128]{1,0:T(8,128)} %param.10) | copy-start | bytes 98308
  0.7 22.8 %copy-start.4 = (f32[64,128]{1,0:T(8,128)S(1)}, f32[64,128]{1,0:T(8,128)}, u32[]{:S(2)}) copy-start(f32[64,128]{1,0:T(8,128)} %param.12) | copy-start | bytes 98308
  0.7 22.9 %copy-start.2 = (f32[64,128]{1,0:T(8,128)S(1)}, f32[64,128]{1,0:T(8,128)}, u32[]{:S(2)}) copy-start(f32[64,128]{1,0:T(8,128)} %param.9) | copy-start | bytes 98308
  0.7 22.9 %copy-start.3 = (f32[64,128]{1,0:T(8,128)S(1)}, f32[64,128]{1,0:T(8,128)}, u32[]{:S(2)}) copy-start(f32[64,128]{1,0:T(8,128)} %param.11) | copy-start | bytes 98308
  1.6 21.9 %collective-permute-start = (f32[2,1,128]{2,1,0:T(1,128)S(1)}, f32[2,1,128]{2,1,0:T(1,128)S(1)}, u32[]{:S(2)}, u32[]{:S(2)}) collective-permute-start(f32[2,1,128]{2,1,0:T(1,128)S(1)} %get-tuple-element.27), channel_id=1, source_target_pairs={{0,4},{4,8},{8,12},{12,16},{16,20},{20,24},{24,28},{28,32},{32,36}... | collective-permute-start | bytes 3080 | tf_op jit(solution)/shard_map/ppermute | solution.py:17
  6.2 17.4 %collective-permute-start.1 = (f32[2,1,128]{2,1,0:T(1,128)S(1)}, f32[2,1,128]{2,1,0:T(1,128)S(1)}, u32[]{:S(2)}, u32[]{:S(2)}) collective-permute-start(f32[2,1,128]{2,1,0:T(1,128)S(1)} %get-tuple-element.28), channel_id=1, source_target_pairs={{4,0},{8,4},{12,8},{16,12},{20,16},{24,20},{28,24},{32,28},{36,32}... | collective-permute-start | bytes 3080 | tf_op jit(solution)/shard_map/ppermute | solution.py:19
  8.8 14.8 %collective-permute-start.2 = (f32[1,128]{1,0:T(1,128)S(1)}, f32[1,128]{1,0:T(1,128)S(1)}, u32[]{:S(2)}, u32[]{:S(2)}) collective-permute-start(f32[1,128]{1,0:T(1,128)S(1)} %get-tuple-element.37), channel_id=1, source_target_pairs={{4,0},{8,4},{12,8},{16,12},{20,16},{24,20},{28,24},{32,28},{36,32}... | collective-permute-start | bytes 1544 | tf_op jit(solution)/shard_map/ppermute | solution.py:19
  10.7 12.9 %collective-permute-start.3 = (f32[1,128]{1,0:T(1,128)S(1)}, f32[1,128]{1,0:T(1,128)S(1)}, u32[]{:S(2)}, u32[]{:S(2)}) collective-permute-start(f32[1,128]{1,0:T(1,128)S(1)} %get-tuple-element.38), channel_id=1, source_target_pairs={{0,4},{4,8},{8,12},{12,16},{16,20},{20,24},{24,28},{28,32},{32,36}... | collective-permute-start | bytes 1544 | tf_op jit(solution)/shard_map/ppermute | solution.py:17
  157.0 13.9 %collective-permute-start.4 = (f32[1,128]{1,0:T(1,128)S(1)}, f32[1,128]{1,0:T(1,128)S(1)}, u32[]{:S(2)}, u32[]{:S(2)}) collective-permute-start(f32[1,128]{1,0:T(1,128)S(1)} %get-tuple-element.35), channel_id=1, source_target_pairs={{4,0},{8,4},{12,8},{16,12},{20,16},{24,20},{28,24},{32,28},{36,32}... | collective-permute-start | bytes 1544 | tf_op jit(solution)/shard_map/ppermute | solution.py:19
  159.6 11.3 %collective-permute-start.5 = (f32[1,128]{1,0:T(1,128)S(1)}, f32[1,128]{1,0:T(1,128)S(1)}, u32[]{:S(2)}, u32[]{:S(2)}) collective-permute-start(f32[1,128]{1,0:T(1,128)S(1)} %get-tuple-element.36), channel_id=1, source_target_pairs={{0,4},{4,8},{8,12},{12,16},{16,20},{20,24},{24,28},{28,32},{32,36}... | collective-permute-start | bytes 1544 | tf_op jit(solution)/shard_map/ppermute | solution.py:17
  301.4 13.9 %collective-permute-start.6 = (f32[1,128]{1,0:T(1,128)S(1)}, f32[1,128]{1,0:T(1,128)S(1)}, u32[]{:S(2)}, u32[]{:S(2)}) collective-permute-start(f32[1,128]{1,0:T(1,128)S(1)} %get-tuple-element.33), channel_id=1, source_target_pairs={{4,0},{8,4},{12,8},{16,12},{20,16},{24,20},{28,24},{32,28},{36,32}... | collective-permute-start | bytes 1544 | tf_op jit(solution)/shard_map/ppermute | solution.py:19
  303.9 11.3 %collective-permute-start.7 = (f32[1,128]{1,0:T(1,128)S(1)}, f32[1,128]{1,0:T(1,128)S(1)}, u32[]{:S(2)}, u32[]{:S(2)}) collective-permute-start(f32[1,128]{1,0:T(1,128)S(1)} %get-tuple-element.34), channel_id=1, source_target_pairs={{0,4},{4,8},{8,12},{12,16},{16,20},{20,24},{24,28},{28,32},{32,36}... | collective-permute-start | bytes 1544 | tf_op jit(solution)/shard_map/ppermute | solution.py:17
  445.7 13.9 %collective-permute-start.8 = (f32[1,128]{1,0:T(1,128)S(1)}, f32[1,128]{1,0:T(1,128)S(1)}, u32[]{:S(2)}, u32[]{:S(2)}) collective-permute-start(f32[1,128]{1,0:T(1,128)S(1)} %get-tuple-element.31), channel_id=1, source_target_pairs={{4,0},{8,4},{12,8},{16,12},{20,16},{24,20},{28,24},{32,28},{36,32}... | collective-permute-start | bytes 1544 | tf_op jit(solution)/shard_map/ppermute | solution.py:19
  448.2 11.3 %collective-permute-start.9 = (f32[1,128]{1,0:T(1,128)S(1)}, f32[1,128]{1,0:T(1,128)S(1)}, u32[]{:S(2)}, u32[]{:S(2)}) collective-permute-start(f32[1,128]{1,0:T(1,128)S(1)} %get-tuple-element.32), channel_id=1, source_target_pairs={{0,4},{4,8},{8,12},{12,16},{16,20},{20,24},{24,28},{28,32},{32,36}... | collective-permute-start | bytes 1544 | tf_op jit(solution)/shard_map/ppermute | solution.py:17
  590.2 13.9 %collective-permute-start.10 = (f32[1,128]{1,0:T(1,128)S(1)}, f32[1,128]{1,0:T(1,128)S(1)}, u32[]{:S(2)}, u32[]{:S(2)}) collective-permute-start(f32[1,128]{1,0:T(1,128)S(1)} %get-tuple-element.29), channel_id=1, source_target_pairs={{4,0},{8,4},{12,8},{16,12},{20,16},{24,20},{28,24},{32,28},{36,32}... | collective-permute-start | bytes 1544 | tf_op jit(solution)/shard_map/ppermute | solution.py:19
  592.7 11.4 %collective-permute-start.11 = (f32[1,128]{1,0:T(1,128)S(1)}, f32[1,128]{1,0:T(1,128)S(1)}, u32[]{:S(2)}, u32[]{:S(2)}) collective-permute-start(f32[1,128]{1,0:T(1,128)S(1)} %get-tuple-element.30), channel_id=1, source_target_pairs={{0,4},{4,8},{8,12},{12,16},{16,20},{20,24},{24,28},{28,32},{32,36}... | collective-permute-start | bytes 1544 | tf_op jit(solution)/shard_map/ppermute | solution.py:17
  595.8 158.6 %copy-start.6 = (f32[64,64]{1,0:T(8,128)S(1)}, f32[64,64]{1,0:T(8,128)}, u32[]{:S(2)}) copy-start(f32[64,64]{1,0:T(8,128)} %param.16) | copy-start | bytes 49156
  668.2 89.7 %copy-start.5 = (f32[64,128]{1,0:T(8,128)}, f32[64,128]{1,0:T(8,128)S(1)}, u32[]{:S(2)}) copy-start(f32[64,128]{1,0:T(8,128)S(1)} %get-tuple-element.7) | copy-start | bytes 98308
where the time goes:
time: 759 us; the launch traced here: 758 us
  blocking collectives  653 us (86%)
  matrix products  48.4 us (6%)
  starting transfers between devices  34.3 us (5%)
  between operations  13 us (2%)
  other arithmetic  8.16 us (1%)
    psum x5, blocking collectives, squares(): return lax.psum(jnp.sum(residual * residual), 'flow')  323 us
    psum x4, blocking collectives, curving(): return lax.psum(jnp.sum(direction * image), 'flow')  248 us
    psum x1, blocking collectives, body(): lax.psum(jnp.dot(pressure.reshape(-1), basis_in, precision=lax.Precision....  67.5 us
    dot_general x5, matrix products, operate(): jnp.einsum('bij,bj->bi', tiles, scale * v, precision=lax.Precision.HIGHEST)  41.5 us
    ppermute x6, starting transfers between devices, extended(): lax.ppermute(tail, axis, [(i, (i + 1) % count) for i in range(ends)])  20.3 us
  transfers between devices with their start and end apart: 12, of which 0 were waited for; matrix products, arithmetic and copies ran while one was open for 6% of the time, Pallas kernels for 0%

commit v1 on v0

v1 whole, which is shorter than its diff:
```python
import functools
import jax
import jax.numpy as jnp
from jax import lax
from jax.experimental import pallas as pl
from jax.experimental.pallas import tpu as pltpu
from jax.sharding import PartitionSpec as P

F32 = jnp.float32
BF16 = jnp.bfloat16
MESH = pl.DeviceIdType.MESH
NV = 5
TOP = 8


def split(x):
    hi = x.astype(BF16)
    return hi, (x - hi.astype(F32)).astype(BF16)


def tile_group(weights, u, g):
    hi, lo = split(u)
    left = jnp.concatenate(
        [jnp.concatenate([hi, hi], 1), jnp.concatenate([lo, jnp.zeros_like(lo)], 1)], 0
    )
    out = jnp.dot(left, weights[g], preferred_element_type=F32)
    rows = [
        out[k : k + 1, k * 128 : k * 128 + 128] + out[8 + k : 9 + k, k * 128 : k * 128 + 128]
        for k in range(8)
    ]
    return jnp.concatenate(rows, axis=0)


def kernel(
    nf, nm, blocks,
    src_h, ap_h, st_h, ge_h, tiles_h, near_h, bin_h, core_h, bout_h,
    p_h, a_h,
    src, ap, st, ge, tiles, weights, near, bin_v, core, bout,
    vec, img, diag, cnext, cprev, scale, p_v, a_v, far, rows,
    h0s, h0r, es, er, m1, m2, m3, mz,
    lsem, tsem, osem, h0sem, esem, bsem, zsem,
):
    me = lax.axis_index("flow")
    owner = lax.axis_index("mech")
    right = lax.rem(me + 1, nf)
    left = lax.rem(me + nf - 1, nf)
    groups = blocks // 8
    chunk = blocks // 4

    loads = []

    def load(i, a, b):
        c = pltpu.make_async_copy(a, b, lsem.at[i])
        c.start()
        loads.append(c)

    load(0, src_h, src)
    load(1, ap_h, ap)
    load(2, ge_h, ge)
    load(3, st_h, st)
    tloads = []
    for q in range(4):
        part = pl.ds(q * chunk, chunk)
        c = pltpu.make_async_copy(tiles_h.at[part], tiles.at[part], tsem.at[q])
        c.start()
        tloads.append(c)
    load(4, bin_h, bin_v)
    load(5, near_h, near)
    load(6, core_h, core)
    load(7, bout_h, bout)

    barrier = pltpu.get_barrier_semaphore()

    def greet(d, carry):
        pl.semaphore_signal(
            barrier, inc=1, device_id={"flow": lax.rem(me + d, nf)}, device_id_type=MESH
        )
        return carry

    lax.fori_loop(1, nf, greet, 0)
    for d in range(1, nm):
        pl.semaphore_signal(
            barrier, inc=1, device_id={"mech": lax.rem(owner + d, nm)}, device_id_type=MESH
        )

    for i in range(3):
        loads[i].wait()
    last = blocks - 1
    h0s[0, 0] = ap[last : last + 1, :]
    h0s[0, 1] = ge[last : last + 1, :]
    h0s[0, 2] = src[last : last + 1, :]
    h0s[1, 0] = ap[0:1, :]
    h0s[1, 1] = ge[0:1, :]
    h0s[1, 2] = src[0:1, :]
    rows[...] = jnp.zeros_like(rows)
    pl.semaphore_wait(barrier, nf - 1 + nm - 1)

    pending = []

    def shift_out(sbuf, rbuf, ssem, rsem):
        out = []
        for side, dev in ((0, right), (1, left)):
            c = pltpu.make_async_remote_copy(
                src_ref=sbuf.at[side],
                dst_ref=rbuf.at[side],
                send_sem=ssem.at[side],
                recv_sem=rsem.at[side],
                device_id={"flow": dev},
                device_id_type=MESH,
            )
            c.start()
            out.append(c)
            pending.append(c)
        return out

    def spread(buf, i):
        def one(d, carry):
            pltpu.make_async_remote_copy(
                src_ref=buf.at[me],
                dst_ref=buf.at[me],
                send_sem=bsem.at[i, 0],
                recv_sem=bsem.at[i, 1],
                device_id={"flow": lax.rem(me + d, nf)},
                device_id_type=MESH,
            ).start()
            return carry

        lax.fori_loop(1, nf, one, 0)

    def gather_wait(buf, i, which):
        others = buf.at[pl.ds(0, nf - 1)]
        pltpu.make_async_copy(others, others, bsem.at[i, which]).wait()

    first_halo = shift_out(h0s, h0r, h0sem.at[0], h0sem.at[1])

    a = ap[...]
    s = a * jnp.sqrt(a)
    scale[...] = s
    b = src[...]
    body = slice(TOP, TOP + blocks)
    above = slice(TOP - 1, TOP - 1 + blocks)
    below = slice(TOP + 1, TOP + 1 + blocks)
    for k in range(NV):
        vec[k, TOP - 1 : TOP, :] = jnp.zeros((1, 128), F32)
        vec[k, TOP + blocks : TOP + blocks + 1, :] = jnp.zeros((1, 128), F32)
    vec[0, body, :] = b

    for q in range(4):
        tloads[q].wait()
        for g in range(q * groups // 4, (q + 1) * groups // 4):
            for k in range(8):
                hi, lo = split(tiles[g * 8 + k])
                weights[g, 0:128, k * 128 : k * 128 + 128] = hi
                weights[g, 128:256, k * 128 : k * 128 + 128] = lo
            part = slice(g * 8, g * 8 + 8)
            img[0, part, :] = tile_group(weights, scale[part, :] * src[part, :], g)

    loads[3].wait()
    for c in first_halo:
        c.wait_recv()
    zero_row = jnp.zeros((1, 128), F32)
    head = me == 0
    tail = me == nf - 1
    ap_next = jnp.where(tail, zero_row, h0r[1, 0])
    cube = a * a * a
    cube_next = jnp.concatenate([cube[1:], ap_next * ap_next * ap_next], axis=0)
    cond = ge[...] * (cube + cube_next) * 0.5
    ap_prev = h0r[0, 0]
    cond_prev = h0r[0, 1] * (ap_prev * ap_prev * ap_prev + cube[0:1]) * 0.5
    cond_prev = jnp.where(head, zero_row, cond_prev)
    cp = jnp.concatenate([cond_prev, cond[:-1]], axis=0)
    cnext[...] = cond
    cprev[...] = cp
    cnext[last : last + 1, :] = jnp.where(tail, zero_row, cond[last:])
    diag[...] = st[...] + cond + cp
    vec[0, TOP - 1 : TOP, :] = h0r[0, 2]
    vec[0, TOP + blocks : TOP + blocks + 1, :] = h0r[1, 2]

    def finish(k):
        img[k] = (
            diag[...] * vec[k, body, :]
            + scale[...] * img[k]
            - cnext[...] * vec[k, below, :]
            - cprev[...] * vec[k, above, :]
        )

    def product(k):
        for g in range(groups):
            part = slice(g * 8, g * 8 + 8)
            u = scale[part, :] * vec[k, TOP + g * 8 : TOP + g * 8 + 8, :]
            img[k, part, :] = tile_group(weights, u, g)

    def send_edges(k, i):
        es[i, 0] = vec[k, TOP + last : TOP + blocks, :]
        es[i, 1] = vec[k, TOP : TOP + 1, :]
        return shift_out(es.at[i], er.at[i], esem.at[i, 0], esem.at[i, 1])

    def patch(copies, k, i):
        for c in copies:
            c.wait_recv()
        img[k, 0:1, :] = img[k, 0:1, :] - cprev[0:1, :] * er[i, 0]
        img[k, last : last + 1, :] = (
            img[k, last : last + 1, :] - cnext[last : last + 1, :] * er[i, 1]
        )

    def dot_row(i, x, y):
        rows[i : i + 1, :] = jnp.sum(x * y, axis=0, keepdims=True)

    def row_sums():
        return jnp.sum(rows[...].T, axis=0, keepdims=True)

    def lane(row, i):
        return jnp.broadcast_to(row[:, i : i + 1], (1, 128))

    finish(0)
    w0 = img[0]
    vec[1, body, :] = w0
    copies = send_edges(1, 0)
    dot_row(0, b, b)
    dot_row(1, b, w0)
    dot_row(2, w0, w0)
    m1[me] = jnp.zeros((1, 128), F32)
    m1[me, 0:1, 0:32] = row_sums()
    spread(m1, 0)
    product(1)
    finish(1)
    patch(copies, 1, 0)

    gather_wait(m1, 0, 1)
    total = jnp.sum(m1[...], axis=0)
    bb, bw, ww = lane(total, 0), lane(total, 1), lane(total, 2)
    mean = bw / bb
    dev = jnp.sqrt(jnp.maximum(ww / bb - mean * mean, (0.01 * mean) * (0.01 * mean)))
    inv = 1.0 / dev
    center = mean + 0.8 * dev
    shifted = center * inv
    w0 = img[0]
    v1 = (w0 - mean * src[...]) * inv
    w1 = (img[1] - mean * w0) * inv
    vec[1, body, :] = v1
    img[1] = w1
    vec[2, body, :] = w1 * inv - shifted * v1 - src[...]
    copies = send_edges(2, 1)
    product(2)
    finish(2)
    b = src[...]
    v2 = vec[2, body, :]
    pairs = {}

    def entry(j, k):
        pairs[(j, k)] = len(pairs)
        dot_row(pairs[(j, k)], vec[k, body, :], img[j])

    def against(k):
        pairs[("g", k)] = len(pairs)
        dot_row(pairs[("g", k)], vec[k, body, :], vec[1, body, :])

    entry(0, 0)
    entry(0, 1)
    entry(1, 1)
    entry(0, 2)
    entry(1, 2)
    against(1)
    against(2)
    patch(copies, 2, 1)
    vec[3, body, :] = img[2] * inv - shifted * v2 - vec[1, body, :]
    copies = send_edges(3, 2)
    product(3)
    finish(3)
    entry(2, 2)
    entry(0, 3)
    entry(1, 3)
    entry(2, 3)
    against(3)
    patch(copies, 3, 2)
    vec[4, body, :] = img[3] * inv - shifted * vec[3, body, :] - v2
    product(4)
    finish(4)
    entry(3, 3)
    for j in range(4):
        entry(j, 4)
    entry(4, 4)
    against(4)
    m2[me, 0] = jnp.zeros((1, 128), F32)
    m2[me, 0, 0:1, 0:32] = row_sums()
    m2[me, 1] = cnext[last : last + 1, :] * vec[4, TOP + last : TOP + blocks, :]
    m2[me, 2] = vec[4, TOP : TOP + 1, :]
    spread(m2, 1)
    loads[4].wait()
    loads[5].wait()
    gather_wait(m2, 1, 1)

    total = jnp.sum(m2[:, 0], axis=0)
    cross = jnp.sum(m2[0 : nf - 1, 1] * m2[1:nf, 2], axis=0)
    cross = jnp.broadcast_to(jnp.sum(cross, axis=1, keepdims=True), (1, 128))
    full = [[None] * NV for _ in range(NV)]
    for j in range(NV):
        for k in range(j, NV):
            full[j][k] = lane(total, pairs[(j, k)])
    full[4][4] = full[4][4] - 2.0 * cross
    size = [full[j][j] for j in range(NV)]
    ratio = -dev / mean
    y = [jnp.zeros((1, 128), F32)] + [ratio * lane(total, pairs[("g", k)]) for k in range(1, NV)]
    low = [[None] * NV for _ in range(NV)]
    pivot = [None] * NV
    for j in range(NV):
        good = full[j][j] > 1e-6 * size[j]
        pivot[j] = jnp.where(good, 1.0 / jnp.where(good, full[j][j], 1.0), 0.0)
        for i in range(j + 1, NV):
            low[i][j] = full[j][i] * pivot[j]
        for i in range(j + 1, NV):
            for k in range(i, NV):
                full[i][k] = full[i][k] - low[i][j] * full[j][k]
            y[i] = y[i] - low[i][j] * y[j]
    coef = [y[j] * pivot[j] for j in range(NV)]
    for j in range(NV - 2, -1, -1):
        for i in range(j + 1, NV):
            coef[j] = coef[j] - low[i][j] * coef[i]
    coef[0] = coef[0] + 1.0 / mean
    p = coef[0] * vec[0, body, :]
    for k in range(1, NV):
        p = p + coef[k] * vec[k, body, :]
    p_v[...] = p
    out_p = pltpu.make_async_copy(p_v, p_h, osem.at[0])
    out_p.start()

    acc = jnp.zeros((64, 128), F32)
    for g in range(blocks):
        acc = acc + bin_v[:, g * 128 : g * 128 + 128] * p_v[g : g + 1, :]
    m3[me] = jnp.zeros((1, 128), F32)
    m3[me, 0:1, 0:64] = jnp.sum(acc.T, axis=0, keepdims=True)
    spread(m3, 2)

    clusters = blocks // nm
    mine = jnp.zeros((clusters, 128), F32)
    for q in range(nm):
        mine = jnp.where(owner == q, p_v[pl.ds(q, clusters, stride=nm), :], mine)
    mine = mine.astype(BF16)
    for c in range(clusters):
        full_c = lax.dot_general(
            mine, near[c], (((1,), (1,)), ((), ())), preferred_element_type=F32
        )
        for q in range(nm):
            mz[owner, nm * c + q : nm * c + q + 1, :] = full_c[c : c + 1, q * 128 : q * 128 + 128]
    for d in range(1, nm):
        c = pltpu.make_async_remote_copy(
            src_ref=mz.at[owner],
            dst_ref=mz.at[owner],
            send_sem=zsem.at[0],
            recv_sem=zsem.at[1],
            device_id={"mech": lax.rem(owner + d, nm)},
            device_id_type=MESH,
        )
        c.start()

    loads[6].wait()
    loads[7].wait()
    gather_wait(m3, 2, 1)
    coeffs = jnp.sum(m3[...], axis=0)[:, 0:64]
    mixed = jnp.sum(core[...] * coeffs, axis=1, keepdims=True)
    mixed = jnp.broadcast_to(mixed, (64, 128))
    for g in range(blocks):
        far[g : g + 1, :] = jnp.sum(
            bout[:, g * 128 : g * 128 + 128] * mixed, axis=0, keepdims=True
        )
    others = mz.at[pl.ds(0, nm - 1)]
    pltpu.make_async_copy(others, others, zsem.at[1]).wait()
    shift = jnp.sum(mz[...], axis=0) + far[...]
    a_v[...] = ap[...] * (1.0 + 0.5 * jnp.tanh(shift))
    out_a = pltpu.make_async_copy(a_v, a_h, osem.at[1])
    out_a.start()
    for c in pending:
        c.wait_send()
    for buf, i in ((m1, 0), (m2, 1), (m3, 2)):
        gather_wait(buf, i, 0)
    pltpu.make_async_copy(others, others, zsem.at[0]).wait()
    out_p.wait()
    out_a.wait()


def solution(mesh):
    nf = mesh.shape["flow"]
    nm = mesh.shape["mech"]

    def local(source, aperture_rest, storage, geometry, tiles, near, basis_in, core, basis_out):
        blocks, width = source.shape
        rank = core.shape[0]
        grid = (blocks, width)
        vm = pltpu.VMEM
        scratch = [
            vm(grid, F32), vm(grid, F32), vm(grid, F32), vm(grid, F32),
            vm(tiles.shape, F32), vm((blocks // 8, 2 * width, 8 * width), BF16),
            vm(near.shape, BF16), vm((rank, basis_in.shape[0]), F32), vm(core.shape, F32),
            vm((rank, basis_in.shape[0]), F32),
            vm((NV, blocks + 2 * TOP, width), F32), vm((NV,) + grid, F32),
            vm(grid, F32), vm(grid, F32), vm(grid, F32), vm(grid, F32),
            vm(grid, F32), vm(grid, F32), vm(grid, F32), vm((32, width), F32),
            vm((2, 3, 1, width), F32), vm((2, 3, 1, width), F32),
            vm((3, 2, 1, width), F32), vm((3, 2, 1, width), F32),
            vm((nf, 1, width), F32), vm((nf, 3, 1, width), F32), vm((nf, 1, width), F32),
            vm((nm,) + grid, F32),
            pltpu.SemaphoreType.DMA((8,)), pltpu.SemaphoreType.DMA((4,)),
            pltpu.SemaphoreType.DMA((2,)), pltpu.SemaphoreType.DMA((2, 2)),
            pltpu.SemaphoreType.DMA((3, 2, 2)), pltpu.SemaphoreType.DMA((3, 2)),
            pltpu.SemaphoreType.DMA((2,)),
        ]
        anywhere = pl.BlockSpec(memory_space=pl.ANY)
        return pl.pallas_call(
            functools.partial(kernel, nf, nm, blocks),
            out_shape=(jax.ShapeDtypeStruct(grid, F32), jax.ShapeDtypeStruct(grid, F32)),
            in_specs=[anywhere] * 9,
            out_specs=(anywhere, anywhere),
            scratch_shapes=scratch,
            compiler_params=pltpu.CompilerParams(
                collective_id=0, has_side_effects=True, vmem_limit_bytes=48 << 20
            ),
        )(
            source, aperture_rest, storage, geometry, tiles, near,
            basis_in.T, core, basis_out.T,
        )

    placed = (
        P("flow", None), P("flow", None), P("flow", None), P("flow", None),
        P("flow", None, None), P("flow", None, "mech"), P("flow", None), P(), P("flow", None),
    )
    return jax.shard_map(
        local,
        mesh=mesh,
        in_specs=placed,
        out_specs=(P("flow", None), P("flow", None)),
        check_vma=False,
    )
```

time: 759 us -> 44.1 us (0.06)
  blocking collectives: 653 us -> 0 us
  matrix products: 48.4 us -> 0 us
  Pallas kernels: 0 us -> 34.7 us
  starting transfers between devices: 34.3 us -> 0 us
  between operations: 13 us -> 0.66 us
  other arithmetic: 8.16 us -> 0 us
    psum x11 -> x0, blocking collectives: 653 us -> none  [the longest x5 323 us: squares(): return lax.psum(jnp.sum(residual * residual), 'flow')]
    dot_general x9 -> x0, matrix products: 48.4 us -> none  [the longest x5 41.5 us: operate(): jnp.einsum('bij,bj->bi', tiles, scale * v, precision=lax.Precision.HIGHEST)]
    pallas_call x0 -> x1, Pallas kernels: none -> 34.7 us  [local(): pl.pallas_call(functools.partial(kernel, nf, nm, blocks), out_shape=(jax....]
    ppermute x12 -> x0, starting transfers between devices: 34.3 us -> none  [the longest x6 20.3 us: extended(): lax.ppermute(tail, axis, [(i, (i + 1) % count) for i in range(ends)])]
    unnamed x14 -> x16, local copies, waits for them, and re-layouts: 0.04 us -> 8.19 us
  transfers between devices with their start and end apart: 12 -> 0, of which waited for: 0 -> 0; matrix products, arithmetic and copies ran while one was open for 6% -> 0% of each run, Pallas kernels for 0% -> 0%
where the time goes in v1:
time: 44.1 us; the launch traced here: 43.6 us
  Pallas kernels  34.7 us (79%)
  local copies, waits for them, and re-layouts  8.19 us (19%)
  between operations  0.66 us (1%)
    pallas_call x1, Pallas kernels, local(): pl.pallas_call(functools.partial(kernel, nf, nm, blocks), out_shape=(jax....  34.7 us
    unnamed x16, local copies, waits for them, and re-layouts  8.19 us

profile of v1, /device:TPU:1, one launch (start us, length us, event | category | flops | bytes accessed | tf_op | source)
XLA Modules:
  0.0 43.6 jit_solution(15411203093466044025)
XLA Ops:
  0.6 0.0 copy-start
  0.6 1.6 %copy-done = bf16[16,512,128]{2,1,0:T(8,128)(2,1)S(1)} copy-done((bf16[16,512,128]{2,1,0:T(8,128)(2,1)S(1)}, bf16[16,512,128]{2,1,0:T(8,128)(2,1)}, u32[]{:S(2)}) %copy-start) | copy-done | bytes 2097176
  2.2 0.0 copy-start.1
  2.2 1.6 %copy-done.1 = f32[8192,64]{0,1:T(8,128)S(1)} copy-done((f32[8192,64]{0,1:T(8,128)S(1)}, f32[8192,64]{0,1:T(8,128)}, u32[]{:S(2)}) %copy-start.1) | copy-done | bytes 2097176
  3.8 0.0 copy-start.2
  3.8 0.8 %copy-done.2 = f32[64,128]{1,0:T(8,128)S(1)} copy-done((f32[64,128]{1,0:T(8,128)S(1)}, f32[64,128]{1,0:T(8,128)}, u32[]{:S(2)}) %copy-start.2) | copy-done | bytes 32792
  4.6 0.0 copy-start.3
  4.6 0.8 %copy-done.3 = f32[64,128]{1,0:T(8,128)S(1)} copy-done((f32[64,128]{1,0:T(8,128)S(1)}, f32[64,128]{1,0:T(8,128)}, u32[]{:S(2)}) %copy-start.3) | copy-done | bytes 32792
  5.3 0.0 copy-start.4
  5.3 0.8 %copy-done.4 = f32[64,128]{1,0:T(8,128)S(1)} copy-done((f32[64,128]{1,0:T(8,128)S(1)}, f32[64,128]{1,0:T(8,128)}, u32[]{:S(2)}) %copy-start.4) | copy-done | bytes 32792
  6.1 0.0 copy-start.5
  6.1 0.8 %copy-done.5 = f32[64,128]{1,0:T(8,128)S(1)} copy-done((f32[64,128]{1,0:T(8,128)S(1)}, f32[64,128]{1,0:T(8,128)}, u32[]{:S(2)}) %copy-start.5) | copy-done | bytes 32792
  6.9 0.0 copy-start.6
  6.9 0.8 %copy-done.6 = f32[64,64]{1,0:T(8,128)S(1)} copy-done((f32[64,64]{1,0:T(8,128)S(1)}, f32[64,64]{1,0:T(8,128)}, u32[]{:S(2)}) %copy-start.6) | copy-done | bytes 16408
  7.6 34.7 %shard_map.104 = (f32[64,128]{1,0:T(8,128)S(1)}, f32[64,128]{1,0:T(8,128)S(1)}) custom-call(f32[64,128]{1,0:T(8,128)S(1)} %copy-done.2, f32[64,128]{1,0:T(8,128)S(1)} %copy-done.3, f32[64,128]{1,0:T(8,128)S(1)} %copy-done.4, f32[64,128]{1,0:T(8,128)S(1)} %copy-done.5, f32[64,128,128]{2,1,0:T(8,128)} %tiles_h.1, bf16[16,512,128]{2,1,0:T(8,128)(2,1)S(1)} %copy-done, ...), custom_call_target="tpu_custom_call" | custom-call | tf_op jit(solution)/shard_map/pallas_call | solution.py:408
  42.3 0.6 %copy.13 = f32[64,128]{1,0:T(8,128)} copy(f32[64,128]{1,0:T(8,128)S(1)} %get-tuple-element.4) | data formatting | bytes 65536
  42.9 0.6 %copy.14 = f32[64,128]{1,0:T(8,128)} copy(f32[64,128]{1,0:T(8,128)S(1)} %get-tuple-element.5) | data formatting | bytes 65536
Async XLA Ops:
  0.6 1.6 %copy-start = (bf16[16,512,128]{2,1,0:T(8,128)(2,1)S(1)}, bf16[16,512,128]{2,1,0:T(8,128)(2,1)}, u32[]{:S(2)}) copy-start(bf16[16,512,128]{2,1,0:T(8,128)(2,1)} %near_h.1) | copy-start | bytes 6291460
  2.2 1.6 %copy-start.1 = (f32[8192,64]{0,1:T(8,128)S(1)}, f32[8192,64]{0,1:T(8,128)}, u32[]{:S(2)}) copy-start(f32[8192,64]{0,1:T(8,128)} %param.15) | copy-start | bytes 6291460
  3.8 0.8 %copy-start.2 = (f32[64,128]{1,0:T(8,128)S(1)}, f32[64,128]{1,0:T(8,128)}, u32[]{:S(2)}) copy-start(f32[64,128]{1,0:T(8,128)} %src_h.1) | copy-start | bytes 98308
  4.6 0.8 %copy-start.3 = (f32[64,128]{1,0:T(8,128)S(1)}, f32[64,128]{1,0:T(8,128)}, u32[]{:S(2)}) copy-start(f32[64,128]{1,0:T(8,128)} %ap_h.1) | copy-start | bytes 98308
  5.3 0.8 %copy-start.4 = (f32[64,128]{1,0:T(8,128)S(1)}, f32[64,128]{1,0:T(8,128)}, u32[]{:S(2)}) copy-start(f32[64,128]{1,0:T(8,128)} %st_h.1) | copy-start | bytes 98308
  6.1 0.8 %copy-start.5 = (f32[64,128]{1,0:T(8,128)S(1)}, f32[64,128]{1,0:T(8,128)}, u32[]{:S(2)}) copy-start(f32[64,128]{1,0:T(8,128)} %ge_h.1) | copy-start | bytes 98308
  6.9 0.8 %copy-start.6 = (f32[64,64]{1,0:T(8,128)S(1)}, f32[64,64]{1,0:T(8,128)}, u32[]{:S(2)}) copy-start(f32[64,64]{1,0:T(8,128)} %core_h.1) | copy-start | bytes 49156

commit v2 on v1

v2 whole, which is shorter than its diff:
```python
import functools
import jax
import jax.numpy as jnp
from jax import lax
from jax.experimental import pallas as pl
from jax.experimental.pallas import tpu as pltpu
from jax.sharding import PartitionSpec as P

F32 = jnp.float32
BF16 = jnp.bfloat16
MESH = pl.DeviceIdType.MESH
NV = 5


def split(x):
    hi = x.astype(BF16)
    return hi, (x - hi.astype(F32)).astype(BF16)


def tile_group(weights, u, g, count=8):
    hi, lo = split(u)
    left = jnp.concatenate(
        [jnp.concatenate([hi, hi], 1), jnp.concatenate([lo, jnp.zeros_like(lo)], 1)], 0
    )
    out = jnp.dot(left, weights[g, :, 0 : count * 128], preferred_element_type=F32)
    rows = [
        out[k : k + 1, k * 128 : k * 128 + 128] + out[8 + k : 9 + k, k * 128 : k * 128 + 128]
        for k in range(count)
    ]
    return jnp.concatenate(rows, axis=0)


def kernel(
    nf, nm, blocks,
    src_h, ap_h, st_h, ge_h, tiles_h, near_h, bin_h, core_h, bout_h,
    p_h, a_h,
    ext, tiles, ghost, weights, near, bin_v, core, bout,
    vec, img, diag, cnext, cprev, scale, p_v, a_v, far, rows,
    m1, m2, m3, mz,
    lsem, tsem, osem, xsem, bsem, zsem,
):
    me = lax.axis_index("flow")
    owner = lax.axis_index("mech")
    right = lax.rem(me + 1, nf)
    left = lax.rem(me + nf - 1, nf)
    head = me == 0
    tail = me == nf - 1
    groups = blocks // 8
    chunk = blocks // 4
    last = blocks - 1
    own = slice(8, 8 + blocks)
    wide = blocks + 16
    body = slice(8, 8 + wide)
    above = slice(7, 7 + wide)
    below = slice(9, 9 + wide)
    mid = slice(16, 16 + blocks)
    zero_row = jnp.zeros((1, 128), F32)

    loads = []

    def load(i, a, b):
        c = pltpu.make_async_copy(a, b, lsem.at[i])
        c.start()
        loads.append(c)

    for i, ref in enumerate((src_h, ap_h, ge_h, st_h)):
        load(i, ref, ext.at[i, pl.ds(8, blocks)])
    tloads = []
    for q in range(4):
        part = pl.ds(q * chunk, chunk)
        c = pltpu.make_async_copy(tiles_h.at[part], tiles.at[part], tsem.at[q])
        c.start()
        tloads.append(c)
    load(4, bin_h, bin_v)
    load(5, near_h, near)
    load(6, core_h, core)
    load(7, bout_h, bout)

    barrier = pltpu.get_barrier_semaphore()

    def greet(d, carry):
        pl.semaphore_signal(
            barrier, inc=1, device_id={"flow": lax.rem(me + d, nf)}, device_id_type=MESH
        )
        return carry

    lax.fori_loop(1, nf, greet, 0)
    for d in range(1, nm):
        pl.semaphore_signal(
            barrier, inc=1, device_id={"mech": lax.rem(owner + d, nm)}, device_id_type=MESH
        )

    def spread(buf, i, size):
        mine = buf.at[pl.ds(pl.multiple_of(me * size, size), size)] if size > 1 else buf.at[me]

        def one(d, carry):
            pltpu.make_async_remote_copy(
                src_ref=mine,
                dst_ref=mine,
                send_sem=bsem.at[i, 0],
                recv_sem=bsem.at[i, 1],
                device_id={"flow": lax.rem(me + d, nf)},
                device_id_type=MESH,
            ).start()
            return carry

        lax.fori_loop(1, nf, one, 0)

    def gather_wait(buf, i, which, size):
        others = buf.at[pl.ds(0, (nf - 1) * size)]
        pltpu.make_async_copy(others, others, bsem.at[i, which]).wait()

    def slots(buf, row):
        return buf[pl.ds(row, nf, stride=8), :]

    def spot(size):
        return pl.ds(pl.multiple_of(me * size, size), size)

    def dot_row(i, x, y):
        rows[i : i + 1, :] = jnp.sum(x * y, axis=0, keepdims=True)

    def row_sums():
        sums = jnp.sum(rows[...].T, axis=0, keepdims=True)
        return jnp.concatenate([sums, jnp.zeros((1, 96), F32)], axis=1)

    def lane(row, i):
        return jnp.broadcast_to(row[:, i : i + 1], (1, 128))

    def total_of(x):
        x = jnp.sum(x, axis=0, keepdims=True)
        return jnp.broadcast_to(jnp.sum(x, axis=1, keepdims=True), (1, 128))

    rows[...] = jnp.zeros_like(rows)
    m1[pl.ds(nf * 8, 8), :] = jnp.zeros((8, 128), F32)
    m2[pl.ds(nf * 8, 8), :] = jnp.zeros((8, 128), F32)
    for k in range(NV):
        vec[k, 0:8, :] = jnp.zeros((8, 128), F32)
        vec[k, 8 + wide : 16 + wide, :] = jnp.zeros((8, 128), F32)
        img[k, 0:8, :] = jnp.zeros((8, 128), F32)
        img[k, 8 + blocks : wide, :] = jnp.zeros((8, 128), F32)

    for i in range(3):
        loads[i].wait()
    a = ext[1, own, :]
    b = ext[0, own, :]
    s = a * jnp.sqrt(a)
    scale[own, :] = s

    def prepare(tile, g, k):
        hi, lo = split(tile)
        weights[g, 0:128, k * 128 : k * 128 + 128] = hi
        weights[g, 128:256, k * 128 : k * 128 + 128] = lo

    for q in range(4):
        tloads[q].wait()
        for g in range(q * groups // 4, (q + 1) * groups // 4):
            for k in range(8):
                prepare(tiles[g * 8 + k], g, k)
            part = slice(8 + g * 8, 16 + g * 8)
            ext[4, part, :] = tile_group(weights, scale[part, :] * ext[0, part, :], g)

    loads[3].wait()
    cube = a * a * a
    half = ext[2, own, :] * 0.5
    edge = half[last:] * cube[last:]
    inner = half[:last] * (cube[:last] + cube[1:])
    cond = jnp.concatenate([inner, jnp.where(tail, edge, zero_row)], axis=0)
    cp = jnp.concatenate([zero_row, inner], axis=0)
    ahead = jnp.concatenate([b[1:], zero_row], axis=0)
    behind = jnp.concatenate([zero_row, b[:last]], axis=0)
    alone = (ext[3, own, :] + cond + cp) * b + s * ext[4, own, :] - cond * ahead - cp * behind
    dot_row(0, b, b)
    dot_row(1, b, alone)
    dot_row(2, alone, alone)
    m1[spot(8), :] = jnp.concatenate(
        [
            row_sums(),
            jnp.where(tail, zero_row, half[last:]), cube[last:], b[last:], alone[last:],
            cube[0:1], b[0:1], alone[0:1],
        ],
        axis=0,
    )
    pl.semaphore_wait(barrier, nf - 1 + nm - 1)

    pending = []

    def hand_over(a, b, i, dev):
        c = pltpu.make_async_remote_copy(
            src_ref=a, dst_ref=b, send_sem=xsem.at[i, 0], recv_sem=xsem.at[i, 1],
            device_id={"flow": dev}, device_id_type=MESH,
        )
        c.start()
        pending.append(c)

    hand_over(ext.at[:, pl.ds(blocks, 8)], ext.at[:, pl.ds(0, 8)], 0, right)
    hand_over(ext.at[:, pl.ds(8, 8)], ext.at[:, pl.ds(8 + blocks, 8)], 1, left)
    hand_over(tiles.at[pl.ds(blocks - 2, 2)], ghost.at[pl.ds(0, 2)], 2, right)
    hand_over(tiles.at[pl.ds(0, 2)], ghost.at[pl.ds(2, 2)], 3, left)
    spread(m1, 0, 8)
    pending[0].wait_recv()
    pending[1].wait_recv()

    row = lax.broadcasted_iota(jnp.int32, (wide, 128), 0)
    at_tail = row == jnp.where(tail, 7 + blocks, -1)
    at_head = row == jnp.where(head, 7, -1)
    a = ext[1]
    s = a * jnp.sqrt(a)
    scale[...] = s
    cube = a * a * a
    cube_next = jnp.where(at_tail, 0.0, jnp.concatenate([cube[1:], zero_row], axis=0))
    cond = jnp.where(at_head, 0.0, ext[2] * (cube + cube_next) * 0.5)
    cp = jnp.concatenate([zero_row, cond[:-1]], axis=0)
    cnext[...] = jnp.where(at_tail, 0.0, cond)
    cprev[...] = cp
    diag[...] = ext[3] + cond + cp
    vec[0, body, :] = ext[0]
    img[0] = ext[4]

    def finish(k):
        img[k] = (
            diag[...] * vec[k, body, :]
            + scale[...] * img[k]
            - cnext[...] * vec[k, below, :]
            - cprev[...] * vec[k, above, :]
        )

    def product(k):
        for g in range(groups):
            part = slice(8 + g * 8, 16 + g * 8)
            u = scale[part, :] * vec[k, 16 + g * 8 : 24 + g * 8, :]
            img[k, part, :] = tile_group(weights, u, g)

    def ghost_product(k):
        low, high = slice(6, 8), slice(8 + blocks, 10 + blocks)
        u = jnp.concatenate(
            [
                scale[low, :] * vec[k, 14:16, :],
                scale[high, :] * vec[k, 16 + blocks : 18 + blocks, :],
                jnp.zeros((4, 128), F32),
            ],
            axis=0,
        )
        out = tile_group(weights, u, groups, 4)
        img[k, low, :] = out[0:2]
        img[k, high, :] = out[2:4]

    finish(0)
    vec[1, body, :] = img[0]
    product(1)
    pending[2].wait_recv()
    pending[3].wait_recv()
    for k in range(4):
        prepare(ghost[k], groups, k)
    ghost_product(1)
    finish(1)
    gather_wait(m1, 0, 1, 8)

    def following(row):
        return m1[pl.ds(8 + row, nf, stride=8), :]

    total = jnp.sum(slots(m1, 0), axis=0, keepdims=True)
    gap = slots(m1, 3) - following(6)
    flux = slots(m1, 1) * (slots(m1, 2) + following(5)) * gap
    bb = lane(total, 0)
    bw = lane(total, 1) + total_of(flux * gap)
    ww = lane(total, 2) + 2.0 * total_of(flux * (slots(m1, 4) - following(7) + flux))
    mean = bw / bb
    dev = jnp.sqrt(jnp.maximum(ww / bb - mean * mean, (0.01 * mean) * (0.01 * mean)))
    inv = 1.0 / dev
    shifted = (mean + 0.8 * dev) * inv
    w0 = img[0]
    b = ext[0]
    v1 = (w0 - mean * b) * inv
    w1 = (img[1] - mean * w0) * inv
    vec[1, body, :] = v1
    img[1] = w1
    vec[2, body, :] = w1 * inv - shifted * v1 - b
    product(2)
    ghost_product(2)
    finish(2)
    vec[3, body, :] = img[2] * inv - shifted * vec[2, body, :] - vec[1, body, :]
    product(3)
    finish(3)
    vec[4, mid, :] = (
        img[3, own, :] * inv - shifted * vec[3, mid, :] - vec[2, mid, :]
    )
    vec[4, 8:16, :] = jnp.zeros((8, 128), F32)
    vec[4, 16 + blocks : 24 + blocks, :] = jnp.zeros((8, 128), F32)
    product(4)
    finish(4)
    pairs = {}

    def entry(j, k):
        pairs[(j, k)] = len(pairs)
        dot_row(pairs[(j, k)], vec[k, mid, :], img[j, own, :])

    for k in range(NV):
        for j in range(k + 1):
            entry(j, k)
    for k in range(1, NV):
        pairs[("g", k)] = len(pairs)
        dot_row(pairs[("g", k)], vec[k, mid, :], vec[1, mid, :])
    m2[spot(8), :] = jnp.concatenate(
        [
            row_sums(),
            cnext[7 + blocks : 8 + blocks, :] * vec[4, 15 + blocks : 16 + blocks, :],
            vec[4, 16:17, :],
            jnp.zeros((5, 128), F32),
        ],
        axis=0,
    )
    spread(m2, 1, 8)
    loads[4].wait()
    loads[5].wait()
    gather_wait(m2, 1, 1, 8)

    total = jnp.sum(slots(m2, 0), axis=0, keepdims=True)
    cross = total_of(slots(m2, 1) * m2[pl.ds(8 + 2, nf, stride=8), :])
    full = [[None] * NV for _ in range(NV)]
    for j in range(NV):
        for k in range(j, NV):
            full[j][k] = lane(total, pairs[(j, k)])
    full[4][4] = full[4][4] - 2.0 * cross
    size = [full[j][j] for j in range(NV)]
    ratio = -dev / mean
    y = [zero_row] + [ratio * lane(total, pairs[("g", k)]) for k in range(1, NV)]
    low = [[None] * NV for _ in range(NV)]
    pivot = [None] * NV
    for j in range(NV):
        good = full[j][j] > 1e-6 * size[j]
        pivot[j] = jnp.where(good, 1.0 / jnp.where(good, full[j][j], 1.0), 0.0)
        for i in range(j + 1, NV):
            low[i][j] = full[j][i] * pivot[j]
        for i in range(j + 1, NV):
            for k in range(i, NV):
                full[i][k] = full[i][k] - low[i][j] * full[j][k]
            y[i] = y[i] - low[i][j] * y[j]
    coef = [y[j] * pivot[j] for j in range(NV)]
    for j in range(NV - 2, -1, -1):
        for i in range(j + 1, NV):
            coef[j] = coef[j] - low[i][j] * coef[i]
    coef[0] = coef[0] + 1.0 / mean
    p = coef[0] * vec[0, mid, :]
    for k in range(1, NV):
        p = p + coef[k] * vec[k, mid, :]
    p_v[...] = p
    out_p = pltpu.make_async_copy(p_v, p_h, osem.at[0])
    out_p.start()

    acc = jnp.zeros((64, 128), F32)
    for g in range(blocks):
        acc = acc + bin_v[:, g * 128 : g * 128 + 128] * p_v[g : g + 1, :]
    m3[me] = jnp.concatenate(
        [jnp.sum(acc.T, axis=0, keepdims=True), jnp.zeros((1, 64), F32)], axis=1
    )
    spread(m3, 2, 1)

    clusters = blocks // nm
    mine = jnp.zeros((clusters, 128), F32)
    for q in range(nm):
        mine = jnp.where(owner == q, p_v[pl.ds(q, clusters, stride=nm), :], mine)
    mine = mine.astype(BF16)
    per = clusters // 4
    for r in range(4):
        for c in range(r * per, (r + 1) * per):
            full_c = lax.dot_general(
                mine, near[c], (((1,), (1,)), ((), ())), preferred_element_type=F32
            )
            for q in range(nm):
                mz[owner, nm * c + q : nm * c + q + 1, :] = full_c[
                    c : c + 1, q * 128 : q * 128 + 128
                ]
        piece = mz.at[owner, pl.ds(r * per * nm, per * nm)]
        for d in range(1, nm):
            pltpu.make_async_remote_copy(
                src_ref=piece,
                dst_ref=piece,
                send_sem=zsem.at[r, 0],
                recv_sem=zsem.at[r, 1],
                device_id={"mech": lax.rem(owner + d, nm)},
                device_id_type=MESH,
            ).start()

    def z_wait(r, which):
        others = mz.at[pl.ds(0, nm - 1), pl.ds(r * per * nm, per * nm)]
        pltpu.make_async_copy(others, others, zsem.at[r, which]).wait()

    loads[6].wait()
    loads[7].wait()
    gather_wait(m3, 2, 1, 1)
    coeffs = jnp.sum(m3[...], axis=0)[:, 0:64]
    mixed = jnp.sum(core[...] * coeffs, axis=1, keepdims=True)
    mixed = jnp.broadcast_to(mixed, (64, 128))
    for g in range(blocks):
        far[g : g + 1, :] = jnp.sum(
            bout[:, g * 128 : g * 128 + 128] * mixed, axis=0, keepdims=True
        )
    for r in range(4):
        z_wait(r, 1)
    shift = jnp.sum(mz[...], axis=0) + far[...]
    a_v[...] = ext[1, own, :] * (1.0 + 0.5 * jnp.tanh(shift))
    out_a = pltpu.make_async_copy(a_v, a_h, osem.at[1])
    out_a.start()
    for c in pending:
        c.wait_send()
    gather_wait(m1, 0, 0, 8)
    gather_wait(m2, 1, 0, 8)
    gather_wait(m3, 2, 0, 1)
    for r in range(4):
        z_wait(r, 0)
    out_p.wait()
    out_a.wait()


def solution(mesh):
    nf = mesh.shape["flow"]
    nm = mesh.shape["mech"]

    def local(source, aperture_rest, storage, geometry, tiles, near, basis_in, core, basis_out):
        blocks, width = source.shape
        rank = core.shape[0]
        grid = (blocks, width)
        vm = pltpu.VMEM
        wide = (blocks + 16, width)
        scratch = [
            vm((5,) + wide, F32), vm(tiles.shape, F32), vm((4, width, width), F32),
            vm((blocks // 8 + 1, 2 * width, 8 * width), BF16),
            vm(near.shape, BF16), vm((rank, basis_in.shape[0]), F32), vm(core.shape, F32),
            vm((rank, basis_in.shape[0]), F32),
            vm((NV, blocks + 32, width), F32), vm((NV,) + wide, F32),
            vm(wide, F32), vm(wide, F32), vm(wide, F32), vm(wide, F32),
            vm(grid, F32), vm(grid, F32), vm(grid, F32), vm((32, width), F32),
            vm(((nf + 1) * 8, width), F32), vm(((nf + 1) * 8, width), F32),
            vm((nf, 1, width), F32), vm((nm,) + grid, F32),
            pltpu.SemaphoreType.DMA((8,)), pltpu.SemaphoreType.DMA((4,)),
            pltpu.SemaphoreType.DMA((2,)), pltpu.SemaphoreType.DMA((4, 2)),
            pltpu.SemaphoreType.DMA((3, 2)), pltpu.SemaphoreType.DMA((4, 2)),
        ]
        anywhere = pl.BlockSpec(memory_space=pltpu.HBM)
        return pl.pallas_call(
            functools.partial(kernel, nf, nm, blocks),
            out_shape=(jax.ShapeDtypeStruct(grid, F32), jax.ShapeDtypeStruct(grid, F32)),
            in_specs=[anywhere] * 9,
            out_specs=(anywhere, anywhere),
            scratch_shapes=scratch,
            compiler_params=pltpu.CompilerParams(
                collective_id=0, has_side_effects=True, vmem_limit_bytes=63 << 20
            ),
        )(
            source, aperture_rest, storage, geometry, tiles, near,
            basis_in.T, core, basis_out.T,
        )

    placed = (
        P("flow", None), P("flow", None), P("flow", None), P("flow", None),
        P("flow", None, None), P("flow", None, "mech"), P("flow", None), P(), P("flow", None),
    )
    return jax.shard_map(
        local,
        mesh=mesh,
        in_specs=placed,
        out_specs=(P("flow", None), P("flow", None)),
        check_vma=False,
    )
```

time: 44.1 us -> 32.7 us (0.74)
  Pallas kernels: 34.7 us -> 29 us
  local copies, waits for them, and re-layouts: 8.19 us -> 2.75 us
    pallas_call x1, Pallas kernels: 34.7 us -> 29 us  [local(): pl.pallas_call(functools.partial(kernel, nf, nm, blocks), out_shape=(jax....]
    unnamed x16 -> x2, local copies, waits for them, and re-layouts: 8.19 us -> 2.75 us
where the time goes in v2:
time: 32.7 us; the launch traced here: 32.4 us
  Pallas kernels  29 us (89%)
  local copies, waits for them, and re-layouts  2.75 us (8%)
  between operations  0.64 us (2%)
    pallas_call x1, Pallas kernels, local(): pl.pallas_call(functools.partial(kernel, nf, nm, blocks), out_shape=(jax....  29 us
    unnamed x2, local copies, waits for them, and re-layouts  2.75 us

profile of v2, /device:TPU:1, one launch (start us, length us, event | category | flops | bytes accessed | tf_op | source)
XLA Modules:
  0.0 32.4 jit_solution(1183510571685627156)
XLA Ops:
  0.6 29.0 %shard_map.104 = (f32[64,128]{1,0:T(8,128)}, f32[64,128]{1,0:T(8,128)}) custom-call(f32[64,128]{1,0:T(8,128)} %src_h.1, f32[64,128]{1,0:T(8,128)} %ap_h.1, f32[64,128]{1,0:T(8,128)} %st_h.1, f32[64,128]{1,0:T(8,128)} %ge_h.1, f32[64,128,128]{2,1,0:T(8,128)} %tiles_h.1, bf16[16,512,128]{2,1,0:T(8,128)(2,1)} %near_h.1, f32[64,8192]{1,0:T(8,128)} %bitcast.2, ...), custom_call_target="tpu_custom_call" | custom-call | tf_op jit(solution)/shard_map/pallas_call | solution.py:440
  29.7 1.4 %copy.13 = f32[64,128]{1,0:T(8,128)} copy(f32[64,128]{1,0:T(8,128)} %get-tuple-element.4) | data formatting | bytes 65536
  31.0 1.4 %copy.14 = f32[64,128]{1,0:T(8,128)} copy(f32[64,128]{1,0:T(8,128)} %get-tuple-element.5) | data formatting | bytes 65536

commit v3 on v2

--- a/solution.py
+++ b/solution.py
@@ -28,6 +28,11 @@
         for k in range(count)
     ]
     return jnp.concatenate(rows, axis=0)
+
+
+def closing(p_in, shift, rest, p_out, a_out):
+    p_out[...] = p_in[...]
+    a_out[...] = rest[...] * (1.0 + 0.5 * jnp.tanh(shift[...]))
 
 
 def kernel(
@@ -194,9 +199,9 @@
 
     hand_over(ext.at[:, pl.ds(blocks, 8)], ext.at[:, pl.ds(0, 8)], 0, right)
     hand_over(ext.at[:, pl.ds(8, 8)], ext.at[:, pl.ds(8 + blocks, 8)], 1, left)
+    spread(m1, 0, 8)
     hand_over(tiles.at[pl.ds(blocks - 2, 2)], ghost.at[pl.ds(0, 2)], 2, right)
     hand_over(tiles.at[pl.ds(0, 2)], ghost.at[pl.ds(2, 2)], 3, left)
-    spread(m1, 0, 8)
     pending[0].wait_recv()
     pending[1].wait_recv()
 
@@ -312,6 +317,17 @@
     spread(m2, 1, 8)
     loads[4].wait()
     loads[5].wait()
+    accs = [jnp.zeros((64, 128), F32)] * NV
+    for g in range(blocks):
+        cut = bin_v[:, g * 128 : g * 128 + 128]
+        accs = [accs[k] + cut * vec[k, 16 + g : 17 + g, :] for k in range(NV)]
+    far_rows = [jnp.sum(acc.T, axis=0, keepdims=True) for acc in accs] + [zero_row[:, 0:64]]
+    m3[spot(8), :] = jnp.concatenate(
+        [jnp.concatenate(far_rows[i : i + 2], axis=1) for i in (0, 2, 4)]
+        + [jnp.zeros((5, 128), F32)],
+        axis=0,
+    )
+    spread(m3, 2, 8)
     gather_wait(m2, 1, 1, 8)
 
     total = jnp.sum(slots(m2, 0), axis=0, keepdims=True)
@@ -347,14 +363,6 @@
     out_p = pltpu.make_async_copy(p_v, p_h, osem.at[0])
     out_p.start()
 
-    acc = jnp.zeros((64, 128), F32)
-    for g in range(blocks):
-        acc = acc + bin_v[:, g * 128 : g * 128 + 128] * p_v[g : g + 1, :]
-    m3[me] = jnp.concatenate(
-        [jnp.sum(acc.T, axis=0, keepdims=True), jnp.zeros((1, 64), F32)], axis=1
-    )
-    spread(m3, 2, 1)
-
     clusters = blocks // nm
     mine = jnp.zeros((clusters, 128), F32)
     for q in range(nm):
@@ -380,15 +388,21 @@
                 device_id={"mech": lax.rem(owner + d, nm)},
                 device_id_type=MESH,
             ).start()
-
     def z_wait(r, which):
         others = mz.at[pl.ds(0, nm - 1), pl.ds(r * per * nm, per * nm)]
         pltpu.make_async_copy(others, others, zsem.at[r, which]).wait()
 
     loads[6].wait()
     loads[7].wait()
-    gather_wait(m3, 2, 1, 1)
-    coeffs = jnp.sum(m3[...], axis=0)[:, 0:64]
+    gather_wait(m3, 2, 1, 8)
+    lower = lax.broadcasted_iota(jnp.int32, (1, 128), 1) < 64
+    parts = [jnp.sum(slots(m3, i), axis=0, keepdims=True) for i in range(3)]
+    both = (
+        jnp.where(lower, coef[0], coef[1]) * parts[0]
+        + jnp.where(lower, coef[2], coef[3]) * parts[1]
+        + coef[4] * parts[2]
+    )
+    coeffs = both[:, 0:64] + both[:, 64:128]
     mixed = jnp.sum(core[...] * coeffs, axis=1, keepdims=True)
     mixed = jnp.broadcast_to(mixed, (64, 128))
     for g in range(blocks):
@@ -397,15 +411,14 @@
         )
     for r in range(4):
         z_wait(r, 1)
-    shift = jnp.sum(mz[...], axis=0) + far[...]
-    a_v[...] = ext[1, own, :] * (1.0 + 0.5 * jnp.tanh(shift))
+    a_v[...] = jnp.sum(mz[...], axis=0) + far[...]
     out_a = pltpu.make_async_copy(a_v, a_h, osem.at[1])
     out_a.start()
     for c in pending:
         c.wait_send()
     gather_wait(m1, 0, 0, 8)
     gather_wait(m2, 1, 0, 8)
-    gather_wait(m3, 2, 0, 1)
+    gather_wait(m3, 2, 0, 8)
     for r in range(4):
         z_wait(r, 0)
     out_p.wait()
@@ -431,13 +444,13 @@
             vm(wide, F32), vm(wide, F32), vm(wide, F32), vm(wide, F32),
             vm(grid, F32), vm(grid, F32), vm(grid, F32), vm((32, width), F32),
             vm(((nf + 1) * 8, width), F32), vm(((nf + 1) * 8, width), F32),
-            vm((nf, 1, width), F32), vm((nm,) + grid, F32),
+            vm((nf * 8, width), F32), vm((nm,) + grid, F32),
             pltpu.SemaphoreType.DMA((8,)), pltpu.SemaphoreType.DMA((4,)),
             pltpu.SemaphoreType.DMA((2,)), pltpu.SemaphoreType.DMA((4, 2)),
             pltpu.SemaphoreType.DMA((3, 2)), pltpu.SemaphoreType.DMA((4, 2)),
         ]
         anywhere = pl.BlockSpec(memory_space=pltpu.HBM)
-        return pl.pallas_call(
+        pressure, shift = pl.pallas_call(
             functools.partial(kernel, nf, nm, blocks),
             out_shape=(jax.ShapeDtypeStruct(grid, F32), jax.ShapeDtypeStruct(grid, F32)),
             in_specs=[anywhere] * 9,
@@ -450,6 +463,12 @@
             source, aperture_rest, storage, geometry, tiles, near,
             basis_in.T, core, basis_out.T,
         )
+        return pl.pallas_call(
+            closing,
+            out_shape=(jax.ShapeDtypeStruct(grid, F32), jax.ShapeDtypeStruct(grid, F32)),
+            in_specs=[pl.BlockSpec(memory_space=pltpu.VMEM)] * 3,
+            out_specs=(pl.BlockSpec(memory_space=pltpu.VMEM),) * 2,
+        )(pressure, shift, aperture_rest)
 
     placed = (
         P("flow", None), P("flow", None), P("flow", None), P("flow", None),

time: 32.7 us -> 29.8 us (0.911)
  local copies, waits for them, and re-layouts: 2.75 us -> 0 us
    unnamed x2 -> x0, local copies, waits for them, and re-layouts: 2.75 us -> none
    pallas_call x0 -> x1, Pallas kernels: none -> 1.42 us  [local(): pl.pallas_call(closing, out_shape=(jax.ShapeDtypeStruct(grid, F32), jax.S...]
    pallas_call x1, Pallas kernels: 29 us -> 27.6 us  [local(): pl.pallas_call(functools.partial(kernel, nf, nm, blocks), out_shape=(jax....]
where the time goes in v3:
time: 29.8 us; the launch traced here: 29.7 us
  Pallas kernels  29 us (97%)
  between operations  0.64 us (2%)
    pallas_call x1, Pallas kernels, local(): pl.pallas_call(functools.partial(kernel, nf, nm, blocks), out_shape=(jax....  27.6 us
    pallas_call x1, Pallas kernels, local(): pl.pallas_call(closing, out_shape=(jax.ShapeDtypeStruct(grid, F32), jax.S...  1.42 us

profile of v3, /device:TPU:1, one launch (start us, length us, event | category | flops | bytes accessed | tf_op | source)
XLA Modules:
  0.0 29.7 jit_solution(15386534087095271892)
XLA Ops:
  0.6 27.6 %shard_map.104 = (f32[64,128]{1,0:T(8,128)}, f32[64,128]{1,0:T(8,128)}) custom-call(f32[64,128]{1,0:T(8,128)} %src_h.1, f32[64,128]{1,0:T(8,128)} %rest.1, f32[64,128]{1,0:T(8,128)} %st_h.1, f32[64,128]{1,0:T(8,128)} %ge_h.1, f32[64,128,128]{2,1,0:T(8,128)} %tiles_h.1, bf16[16,512,128]{2,1,0:T(8,128)(2,1)} %near_h.1, f32[64,8192]{1,0:T(8,128)} %bitcast.2, ...), custom_call_target="tpu_custom_call" | custom-call | tf_op jit(solution)/shard_map/pallas_call | solution.py:453
  28.2 1.4 %shard_map.105 = (f32[64,128]{1,0:T(8,128)}, f32[64,128]{1,0:T(8,128)}) custom-call(f32[64,128]{1,0:T(8,128)} %get-tuple-element.4.p_in, f32[64,128]{1,0:T(8,128)} %get-tuple-element.5.shift, f32[64,128]{1,0:T(8,128)} %rest.1), custom_call_target="tpu_custom_call" | custom-call | tf_op jit(solution)/shard_map/pallas_call | solution.py:466

commit v4 on v3

--- a/solution.py
+++ b/solution.py
@@ -10,11 +10,97 @@
 BF16 = jnp.bfloat16
 MESH = pl.DeviceIdType.MESH
 NV = 5
+LEAST = 5e-5
 
 
 def split(x):
     hi = x.astype(BF16)
     return hi, (x - hi.astype(F32)).astype(BF16)
+
+
+CG = 5
+
+
+def extended(cells, sides, width):
+    for axis, dim in sides:
+        count = lax.axis_size(axis)
+        ends = count - 1
+        head = lax.slice_in_dim(cells, 0, width, axis=dim)
+        tail = lax.slice_in_dim(cells, cells.shape[dim] - width, cells.shape[dim], axis=dim)
+        cells = jnp.concatenate(
+            [
+                lax.ppermute(tail, axis, [(i, (i + 1) % count) for i in range(ends)]),
+                cells,
+                lax.ppermute(head, axis, [((i + 1) % count, i) for i in range(ends)]),
+            ],
+            axis=dim,
+        )
+    return cells
+
+
+def exchange_faces(v):
+    return extended(v, (("flow", 0),), 1)
+
+
+def operate(v, tiles, scale, storage, cond_all):
+    padded = exchange_faces(v)
+    local = jnp.einsum("bij,bj->bi", tiles, scale * v, precision=lax.Precision.HIGHEST) * scale
+    cond = cond_all[1:]
+    cprv = cond_all[:-1]
+    return storage * v + local + (cond + cprv) * v - cond * padded[2:] - cprv * padded[:-2]
+
+
+def squares(residual):
+    return lax.psum(jnp.sum(residual * residual), "flow")
+
+
+def curving(direction, image):
+    return lax.psum(jnp.sum(direction * image), "flow")
+
+
+def solve_flow(source, tiles, scale, storage, cond_all):
+    pressure = jnp.zeros_like(source)
+    residual = source
+    direction = source
+    norm_now = squares(residual)
+    for step in range(CG):
+        image = operate(direction, tiles, scale, storage, cond_all)
+        alpha = norm_now / curving(direction, image)
+        pressure = pressure + alpha * direction
+        residual = residual - alpha * image
+        norm_next = squares(residual)
+        direction = residual + norm_next / norm_now * direction
+        norm_now = norm_next
+    return pressure
+
+
+def plain(source, aperture_rest, storage, geometry, tiles, near, basis_in, core, basis_out):
+    blocks, width = source.shape
+    groups = lax.axis_size("mech")
+    owner = lax.axis_index("mech")
+    clusters = near.shape[0]
+    span = near.shape[2]
+    aperture = aperture_rest
+    stacked = jnp.stack([aperture, geometry])
+    padded = extended(stacked, (("flow", 1),), 1)
+    ap_pad = padded[0]
+    geo_pad = padded[1]
+    cond_all = geo_pad[:-1] * (ap_pad[:-1] ** 3 + ap_pad[1:] ** 3) * 0.5
+    scale = aperture**1.5
+    pressure = solve_flow(source, tiles, scale, storage, cond_all)
+    packed = pressure.astype(jnp.bfloat16).reshape(clusters, span * groups)
+    piece = lax.dynamic_slice_in_dim(packed, owner * span, span, 1)
+    partial_value = jnp.einsum(
+        "cij,cj->ci", near, piece, preferred_element_type=jnp.float32
+    ).reshape(blocks, width)
+    coeffs = lax.psum(
+        jnp.dot(pressure.reshape(-1), basis_in, precision=lax.Precision.HIGHEST), "flow"
+    )
+    mixed = jnp.dot(core, coeffs, precision=lax.Precision.HIGHEST)
+    near_disp = lax.psum(partial_value, "mech")
+    far_disp = jnp.dot(basis_out, mixed, precision=lax.Precision.HIGHEST).reshape(blocks, width)
+    aperture = aperture_rest * (1.0 + 0.5 * jnp.tanh(near_disp + far_disp))
+    return (pressure, aperture)
 
 
 def tile_group(weights, u, g, count=8):
@@ -38,9 +124,9 @@
 def kernel(
     nf, nm, blocks,
     src_h, ap_h, st_h, ge_h, tiles_h, near_h, bin_h, core_h, bout_h,
-    p_h, a_h,
+    p_h, a_h, f_h,
     ext, tiles, ghost, weights, near, bin_v, core, bout,
-    vec, img, diag, cnext, cprev, scale, p_v, a_v, far, rows,
+    vec, img, diag, cnext, cprev, scale, p_v, a_v, f_v, far, rows,
     m1, m2, m3, mz,
     lsem, tsem, osem, xsem, bsem, zsem,
 ):
@@ -76,10 +162,6 @@
         c = pltpu.make_async_copy(tiles_h.at[part], tiles.at[part], tsem.at[q])
         c.start()
         tloads.append(c)
-    load(4, bin_h, bin_v)
-    load(5, near_h, near)
-    load(6, core_h, core)
-    load(7, bout_h, bout)
 
     barrier = pltpu.get_barrier_semaphore()
 
@@ -96,7 +178,7 @@
         )
 
     def spread(buf, i, size):
-        mine = buf.at[pl.ds(pl.multiple_of(me * size, size), size)] if size > 1 else buf.at[me]
+        mine = buf.at[pl.ds(pl.multiple_of(me * 8, 8), size)]
 
         def one(d, carry):
             pltpu.make_async_remote_copy(
@@ -118,8 +200,8 @@
     def slots(buf, row):
         return buf[pl.ds(row, nf, stride=8), :]
 
-    def spot(size):
-        return pl.ds(pl.multiple_of(me * size, size), size)
+    def spot():
+        return pl.ds(pl.multiple_of(me * 8, 8), 8)
 
     def dot_row(i, x, y):
         rows[i : i + 1, :] = jnp.sum(x * y, axis=0, keepdims=True)
@@ -164,6 +246,10 @@
             part = slice(8 + g * 8, 16 + g * 8)
             ext[4, part, :] = tile_group(weights, scale[part, :] * ext[0, part, :], g)
 
+    load(4, bin_h, bin_v)
+    load(5, near_h, near)
+    load(6, core_h, core)
+    load(7, bout_h, bout)
     loads[3].wait()
     cube = a * a * a
     half = ext[2, own, :] * 0.5
@@ -177,13 +263,11 @@
     dot_row(0, b, b)
     dot_row(1, b, alone)
     dot_row(2, alone, alone)
-    m1[spot(8), :] = jnp.concatenate(
-        [
-            row_sums(),
-            jnp.where(tail, zero_row, half[last:]), cube[last:], b[last:], alone[last:],
-            cube[0:1], b[0:1], alone[0:1],
-        ],
-        axis=0,
+    rows[3:4, :] = jnp.where(tail, zero_row, half[last:]) * (1.0 / 128.0)
+    rows[4:5, :] = cube[last:] * (1.0 / 128.0)
+    rows[5:6, :] = cube[0:1] * (1.0 / 128.0)
+    m1[spot(), :] = jnp.concatenate(
+        [row_sums(), b[last:], b[0:1], jnp.zeros((5, 128), F32)], axis=0
     )
     pl.semaphore_wait(barrier, nf - 1 + nm - 1)
 
@@ -199,7 +283,7 @@
 
     hand_over(ext.at[:, pl.ds(blocks, 8)], ext.at[:, pl.ds(0, 8)], 0, right)
     hand_over(ext.at[:, pl.ds(8, 8)], ext.at[:, pl.ds(8 + blocks, 8)], 1, left)
-    spread(m1, 0, 8)
+    spread(m1, 0, 3)
     hand_over(tiles.at[pl.ds(blocks - 2, 2)], ghost.at[pl.ds(0, 2)], 2, right)
     hand_over(tiles.at[pl.ds(0, 2)], ghost.at[pl.ds(2, 2)], 3, left)
     pending[0].wait_recv()
@@ -258,17 +342,18 @@
         prepare(ghost[k], groups, k)
     ghost_product(1)
     finish(1)
-    gather_wait(m1, 0, 1, 8)
+    gather_wait(m1, 0, 1, 3)
 
     def following(row):
         return m1[pl.ds(8 + row, nf, stride=8), :]
 
-    total = jnp.sum(slots(m1, 0), axis=0, keepdims=True)
-    gap = slots(m1, 3) - following(6)
-    flux = slots(m1, 1) * (slots(m1, 2) + following(5)) * gap
+    sums = slots(m1, 0)
+    total = jnp.sum(sums, axis=0, keepdims=True)
+    gap = slots(m1, 1) - following(2)
+    flux = sums[:, 3:4] * (sums[:, 4:5] + following(0)[:, 5:6]) * gap
     bb = lane(total, 0)
     bw = lane(total, 1) + total_of(flux * gap)
-    ww = lane(total, 2) + 2.0 * total_of(flux * (slots(m1, 4) - following(7) + flux))
+    ww = lane(total, 2) + 2.0 * total_of(flux * (lane(total, 1) / bb * gap + flux))
     mean = bw / bb
     dev = jnp.sqrt(jnp.maximum(ww / bb - mean * mean, (0.01 * mean) * (0.01 * mean)))
     inv = 1.0 / dev
@@ -302,10 +387,10 @@
     for k in range(NV):
         for j in range(k + 1):
             entry(j, k)
-    for k in range(1, NV):
+    for k in range(NV):
         pairs[("g", k)] = len(pairs)
         dot_row(pairs[("g", k)], vec[k, mid, :], vec[1, mid, :])
-    m2[spot(8), :] = jnp.concatenate(
+    m2[spot(), :] = jnp.concatenate(
         [
             row_sums(),
             cnext[7 + blocks : 8 + blocks, :] * vec[4, 15 + blocks : 16 + blocks, :],
@@ -314,7 +399,7 @@
         ],
         axis=0,
     )
-    spread(m2, 1, 8)
+    spread(m2, 1, 3)
     loads[4].wait()
     loads[5].wait()
     accs = [jnp.zeros((64, 128), F32)] * NV
@@ -322,13 +407,13 @@
         cut = bin_v[:, g * 128 : g * 128 + 128]
         accs = [accs[k] + cut * vec[k, 16 + g : 17 + g, :] for k in range(NV)]
     far_rows = [jnp.sum(acc.T, axis=0, keepdims=True) for acc in accs] + [zero_row[:, 0:64]]
-    m3[spot(8), :] = jnp.concatenate(
+    m3[spot(), :] = jnp.concatenate(
         [jnp.concatenate(far_rows[i : i + 2], axis=1) for i in (0, 2, 4)]
         + [jnp.zeros((5, 128), F32)],
         axis=0,
     )
-    spread(m3, 2, 8)
-    gather_wait(m2, 1, 1, 8)
+    spread(m3, 2, 3)
+    gather_wait(m2, 1, 1, 3)
 
     total = jnp.sum(slots(m2, 0), axis=0, keepdims=True)
     cross = total_of(slots(m2, 1) * m2[pl.ds(8 + 2, nf, stride=8), :])
@@ -339,12 +424,14 @@
     full[4][4] = full[4][4] - 2.0 * cross
     size = [full[j][j] for j in range(NV)]
     ratio = -dev / mean
-    y = [zero_row] + [ratio * lane(total, pairs[("g", k)]) for k in range(1, NV)]
+    y = [ratio * lane(total, pairs[("g", k)]) for k in range(NV)]
     low = [[None] * NV for _ in range(NV)]
     pivot = [None] * NV
+    least = None
     for j in range(NV):
-        good = full[j][j] > 1e-6 * size[j]
-        pivot[j] = jnp.where(good, 1.0 / jnp.where(good, full[j][j], 1.0), 0.0)
+        pivot[j] = 1.0 / full[j][j]
+        margin = full[j][j] - LEAST * size[j]
+        least = margin if j == 0 else jnp.minimum(least, margin)
         for i in range(j + 1, NV):
             low[i][j] = full[j][i] * pivot[j]
         for i in range(j + 1, NV):
@@ -360,6 +447,7 @@
     for k in range(1, NV):
         p = p + coef[k] * vec[k, mid, :]
     p_v[...] = p
+    f_h[0, 0] = least[0, 0]
     out_p = pltpu.make_async_copy(p_v, p_h, osem.at[0])
     out_p.start()
 
@@ -394,7 +482,7 @@
 
     loads[6].wait()
     loads[7].wait()
-    gather_wait(m3, 2, 1, 8)
+    gather_wait(m3, 2, 1, 3)
     lower = lax.broadcasted_iota(jnp.int32, (1, 128), 1) < 64
     parts = [jnp.sum(slots(m3, i), axis=0, keepdims=True) for i in range(3)]
     both = (
@@ -416,9 +504,9 @@
     out_a.start()
     for c in pending:
         c.wait_send()
-    gather_wait(m1, 0, 0, 8)
-    gather_wait(m2, 1, 0, 8)
-    gather_wait(m3, 2, 0, 8)
+    gather_wait(m1, 0, 0, 3)
+    gather_wait(m2, 1, 0, 3)
+    gather_wait(m3, 2, 0, 3)
     for r in range(4):
         z_wait(r, 0)
     out_p.wait()
@@ -442,19 +530,23 @@
             vm((rank, basis_in.shape[0]), F32),
             vm((NV, blocks + 32, width), F32), vm((NV,) + wide, F32),
             vm(wide, F32), vm(wide, F32), vm(wide, F32), vm(wide, F32),
-            vm(grid, F32), vm(grid, F32), vm(grid, F32), vm((32, width), F32),
+            vm(grid, F32), vm(grid, F32), vm((8, width), F32), vm(grid, F32), vm((32, width), F32),
             vm(((nf + 1) * 8, width), F32), vm(((nf + 1) * 8, width), F32),
             vm((nf * 8, width), F32), vm((nm,) + grid, F32),
             pltpu.SemaphoreType.DMA((8,)), pltpu.SemaphoreType.DMA((4,)),
-            pltpu.SemaphoreType.DMA((2,)), pltpu.SemaphoreType.DMA((4, 2)),
+            pltpu.SemaphoreType.DMA((3,)), pltpu.SemaphoreType.DMA((4, 2)),
             pltpu.SemaphoreType.DMA((3, 2)), pltpu.SemaphoreType.DMA((4, 2)),
         ]
         anywhere = pl.BlockSpec(memory_space=pltpu.HBM)
-        pressure, shift = pl.pallas_call(
+        pressure, shift, margin = pl.pallas_call(
             functools.partial(kernel, nf, nm, blocks),
-            out_shape=(jax.ShapeDtypeStruct(grid, F32), jax.ShapeDtypeStruct(grid, F32)),
+            out_shape=(
+                jax.ShapeDtypeStruct(grid, F32),
+                jax.ShapeDtypeStruct(grid, F32),
+                jax.ShapeDtypeStruct((1, 1), F32),
+            ),
             in_specs=[anywhere] * 9,
-            out_specs=(anywhere, anywhere),
+            out_specs=(anywhere, anywhere, pl.BlockSpec(memory_space=pltpu.SMEM)),
             scratch_shapes=scratch,
             compiler_params=pltpu.CompilerParams(
                 collective_id=0, has_side_effects=True, vmem_limit_bytes=63 << 20
@@ -463,12 +555,19 @@
             source, aperture_rest, storage, geometry, tiles, near,
             basis_in.T, core, basis_out.T,
         )
-        return pl.pallas_call(
+        end = pl.pallas_call(
             closing,
             out_shape=(jax.ShapeDtypeStruct(grid, F32), jax.ShapeDtypeStruct(grid, F32)),
             in_specs=[pl.BlockSpec(memory_space=pltpu.VMEM)] * 3,
             out_specs=(pl.BlockSpec(memory_space=pltpu.VMEM),) * 2,
-        )(pressure, shift, aperture_rest)
+        )
+        return lax.cond(
+            margin[0, 0] > 0.0,
+            lambda: end(pressure, shift, aperture_rest),
+            lambda: plain(
+                source, aperture_rest, storage, geometry, tiles, near, basis_in, core, basis_out
+            ),
+        )
 
     placed = (
         P("flow", None), P("flow", None), P("flow", None), P("flow", None),

time: 29.8 us -> 29 us (0.973)
  Pallas kernels: 29 us -> 27.2 us
  between operations: 0.64 us -> 1.41 us
    pallas_call x1, Pallas kernels: 27.6 us -> 26.6 us  [local(): pl.pallas_call(functools.partial(kernel, nf, nm, blocks), out_shape=(jax....]
    pallas_call x1, Pallas kernels: 1.42 us -> 0.63 us  [local(): end(pressure, shift, aperture_rest)]
where the time goes in v4:
time: 29 us; the launch traced here: 28.9 us
  Pallas kernels  27.2 us (94%)
  between operations  1.41 us (5%)
    pallas_call x1, Pallas kernels, local(): pl.pallas_call(functools.partial(kernel, nf, nm, blocks), out_shape=(jax....  26.6 us
    pallas_call x1, Pallas kernels, local(): end(pressure, shift, aperture_rest)  0.63 us

profile of v4, /device:TPU:1, one launch (start us, length us, event | category | flops | bytes accessed | tf_op | source)
XLA Modules:
  0.0 28.9 jit_solution(2937899180512618622)
XLA Ops:
  0.6 0.0 copy-start
  0.6 0.0 copy-start.2
  0.7 0.0 copy-start.3
  0.7 0.0 copy-start.4
  0.7 0.0 copy-start.5
  0.7 26.6 %shard_map.106 = (f32[64,128]{1,0:T(8,128)S(1)}, f32[64,128]{1,0:T(8,128)S(1)}, f32[1,1]{1,0:T(1,128)}) custom-call(f32[64,128]{1,0:T(8,128)} %src_h.1, f32[64,128]{1,0:T(8,128)} %ap_h.1, f32[64,128]{1,0:T(8,128)} %st_h.1, f32[64,128]{1,0:T(8,128)} %ge_h.1, f32[64,128,128]{2,1,0:T(8,128)} %tiles_h.1, bf16[16,512,128]{2,1,0:T(8,128)(2,1)} %near_h.1, ...), custom_call_target="tpu_custom_call" | custom-call | tf_op jit(solution)/shard_map/pallas_call | solution.py:541
  27.9 0.0 copy-done
  28.0 0.0 copy-done.2
  28.0 0.0 copy-done.3
  28.0 0.0 copy-done.4
  28.0 0.0 copy-done.5
  28.0 0.9 %conditional.1 = ((f32[64,128]{1,0:T(8,128)}, f32[64,128]{1,0:T(8,128)})) conditional(s32[]{:T(128)} %bitcast.37, (f32[64,128]{1,0:T(8,128)S(1)}, f32[64,128]{1,0:T(8,128)S(1)}, f32[64,128]{1,0:T(8,128)S(1)}, f32[64,128,128]{2,1,0:T(8,128)}, f32[64,128]{1,0:T(8,128)S(1)}, /*index=5*/bf16[16,512,128]{2,1,0:T(8,128)(2,1)}, f32[8192,64]{0,1:T(8,128)}, ...), branch_computations={%region_0.0_spmd, %region_23.0_spmd} | conditional | flops 78751936 | bytes 39485336 | solution.py:564
  28.2 0.6 %branch_1_fun.1 = (f32[64,128]{1,0:T(8,128)}, f32[64,128]{1,0:T(8,128)}) custom-call(f32[64,128]{1,0:T(8,128)S(1)} %get-tuple-element.33.p_in, f32[64,128]{1,0:T(8,128)S(1)} %get-tuple-element.34.shift, f32[64,128]{1,0:T(8,128)S(1)} %get-tuple-element.35.rest), custom_call_target="tpu_custom_call" | custom-call | tf_op jit(solution)/shard_map/cond/branch_1_fun/pallas_call | solution.py:566
Async XLA Ops:
  0.6 27.3 %copy-start = (f32[64,128]{1,0:T(8,128)S(1)}, f32[64,128]{1,0:T(8,128)}, u32[]{:S(2)}) copy-start(f32[64,128]{1,0:T(8,128)} %ap_h.1) | copy-start | bytes 98308
  0.6 27.3 %copy-start.2 = (f32[64,128]{1,0:T(8,128)S(1)}, f32[64,128]{1,0:T(8,128)}, u32[]{:S(2)}) copy-start(f32[64,128]{1,0:T(8,128)} %src_h.1) | copy-start | bytes 98308
  0.7 27.3 %copy-start.3 = (f32[64,128]{1,0:T(8,128)S(1)}, f32[64,128]{1,0:T(8,128)}, u32[]{:S(2)}) copy-start(f32[64,128]{1,0:T(8,128)} %st_h.1) | copy-start | bytes 98308
  0.7 27.3 %copy-start.4 = (f32[64,128]{1,0:T(8,128)S(1)}, f32[64,128]{1,0:T(8,128)}, u32[]{:S(2)}) copy-start(f32[64,128]{1,0:T(8,128)} %ge_h.1) | copy-start | bytes 98308
  0.7 27.3 %copy-start.5 = (f32[64,64]{1,0:T(8,128)S(1)}, f32[64,64]{1,0:T(8,128)}, u32[]{:S(2)}) copy-start(f32[64,64]{1,0:T(8,128)} %core_h.1) | copy-start | bytes 49156

commit v5 on v4

--- a/solution.py
+++ b/solution.py
@@ -260,6 +260,10 @@
     ahead = jnp.concatenate([b[1:], zero_row], axis=0)
     behind = jnp.concatenate([zero_row, b[:last]], axis=0)
     alone = (ext[3, own, :] + cond + cp) * b + s * ext[4, own, :] - cond * ahead - cp * behind
+    img[0, own, :] = alone
+    for g in (0, groups - 1):
+        part = slice(8 + g * 8, 16 + g * 8)
+        ext[5, part, :] = tile_group(weights, scale[part, :] * img[0, part, :], g)
     dot_row(0, b, b)
     dot_row(1, b, alone)
     dot_row(2, alone, alone)
@@ -284,8 +288,8 @@
     hand_over(ext.at[:, pl.ds(blocks, 8)], ext.at[:, pl.ds(0, 8)], 0, right)
     hand_over(ext.at[:, pl.ds(8, 8)], ext.at[:, pl.ds(8 + blocks, 8)], 1, left)
     spread(m1, 0, 3)
-    hand_over(tiles.at[pl.ds(blocks - 2, 2)], ghost.at[pl.ds(0, 2)], 2, right)
-    hand_over(tiles.at[pl.ds(0, 2)], ghost.at[pl.ds(2, 2)], 3, left)
+    hand_over(tiles.at[blocks - 1], ghost.at[0], 2, right)
+    hand_over(tiles.at[0], ghost.at[1], 3, left)
     pending[0].wait_recv()
     pending[1].wait_recv()
 
@@ -320,27 +324,29 @@
             img[k, part, :] = tile_group(weights, u, g)
 
     def ghost_product(k):
-        low, high = slice(6, 8), slice(8 + blocks, 10 + blocks)
+        low, high = slice(7, 8), slice(8 + blocks, 9 + blocks)
         u = jnp.concatenate(
             [
-                scale[low, :] * vec[k, 14:16, :],
-                scale[high, :] * vec[k, 16 + blocks : 18 + blocks, :],
-                jnp.zeros((4, 128), F32),
+                scale[low, :] * vec[k, 15:16, :],
+                scale[high, :] * vec[k, 16 + blocks : 17 + blocks, :],
+                jnp.zeros((6, 128), F32),
             ],
             axis=0,
         )
-        out = tile_group(weights, u, groups, 4)
-        img[k, low, :] = out[0:2]
-        img[k, high, :] = out[2:4]
+        out = tile_group(weights, u, groups, 2)
+        img[k, low, :] = out[0:1]
+        img[k, high, :] = out[1:2]
 
     finish(0)
     vec[1, body, :] = img[0]
     product(1)
     pending[2].wait_recv()
     pending[3].wait_recv()
-    for k in range(4):
+    for k in range(2):
         prepare(ghost[k], groups, k)
     ghost_product(1)
+    img[1, 6:7, :] = ext[5, 6:7, :]
+    img[1, 9 + blocks : 10 + blocks, :] = ext[5, 9 + blocks : 10 + blocks, :]
     finish(1)
     gather_wait(m1, 0, 1, 3)
 
@@ -365,11 +371,28 @@
     vec[1, body, :] = v1
     img[1] = w1
     vec[2, body, :] = w1 * inv - shifted * v1 - b
+    pairs = {}
+
+    def entry(j, k):
+        pairs[(j, k)] = len(pairs)
+        dot_row(pairs[(j, k)], vec[k, mid, :], img[j, own, :])
+
+    def against(k):
+        pairs[("g", k)] = len(pairs)
+        dot_row(pairs[("g", k)], vec[k, mid, :], vec[1, mid, :])
+
     product(2)
     ghost_product(2)
+    for j, k in ((0, 0), (0, 1), (1, 1), (0, 2), (1, 2)):
+        entry(j, k)
+    for k in range(3):
+        against(k)
     finish(2)
     vec[3, body, :] = img[2] * inv - shifted * vec[2, body, :] - vec[1, body, :]
     product(3)
+    for j, k in ((2, 2), (0, 3), (1, 3), (2, 3)):
+        entry(j, k)
+    against(3)
     finish(3)
     vec[4, mid, :] = (
         img[3, own, :] * inv - shifted * vec[3, mid, :] - vec[2, mid, :]
@@ -377,19 +400,11 @@
     vec[4, 8:16, :] = jnp.zeros((8, 128), F32)
     vec[4, 16 + blocks : 24 + blocks, :] = jnp.zeros((8, 128), F32)
     product(4)
+    for j, k in ((3, 3), (0, 4), (1, 4), (2, 4), (3, 4)):
+        entry(j, k)
+    against(4)
     finish(4)
-    pairs = {}
-
-    def entry(j, k):
-        pairs[(j, k)] = len(pairs)
-        dot_row(pairs[(j, k)], vec[k, mid, :], img[j, own, :])
-
-    for k in range(NV):
-        for j in range(k + 1):
-            entry(j, k)
-    for k in range(NV):
-        pairs[("g", k)] = len(pairs)
-        dot_row(pairs[("g", k)], vec[k, mid, :], vec[1, mid, :])
+    entry(4, 4)
     m2[spot(), :] = jnp.concatenate(
         [
             row_sums(),
@@ -448,8 +463,7 @@
         p = p + coef[k] * vec[k, mid, :]
     p_v[...] = p
     f_h[0, 0] = least[0, 0]
-    out_p = pltpu.make_async_copy(p_v, p_h, osem.at[0])
-    out_p.start()
+    p_h[...] = p
 
     clusters = blocks // nm
     mine = jnp.zeros((clusters, 128), F32)
@@ -499,9 +513,7 @@
         )
     for r in range(4):
         z_wait(r, 1)
-    a_v[...] = jnp.sum(mz[...], axis=0) + far[...]
-    out_a = pltpu.make_async_copy(a_v, a_h, osem.at[1])
-    out_a.start()
+    a_h[...] = jnp.sum(mz[...], axis=0) + far[...]
     for c in pending:
         c.wait_send()
     gather_wait(m1, 0, 0, 3)
@@ -509,8 +521,6 @@
     gather_wait(m3, 2, 0, 3)
     for r in range(4):
         z_wait(r, 0)
-    out_p.wait()
-    out_a.wait()
 
 
 def solution(mesh):
@@ -524,7 +534,7 @@
         vm = pltpu.VMEM
         wide = (blocks + 16, width)
         scratch = [
-            vm((5,) + wide, F32), vm(tiles.shape, F32), vm((4, width, width), F32),
+            vm((6,) + wide, F32), vm(tiles.shape, F32), vm((2, width, width), F32),
             vm((blocks // 8 + 1, 2 * width, 8 * width), BF16),
             vm(near.shape, BF16), vm((rank, basis_in.shape[0]), F32), vm(core.shape, F32),
             vm((rank, basis_in.shape[0]), F32),
@@ -546,7 +556,11 @@
                 jax.ShapeDtypeStruct((1, 1), F32),
             ),
             in_specs=[anywhere] * 9,
-            out_specs=(anywhere, anywhere, pl.BlockSpec(memory_space=pltpu.SMEM)),
+            out_specs=(
+                pl.BlockSpec(memory_space=pltpu.VMEM),
+                pl.BlockSpec(memory_space=pltpu.VMEM),
+                pl.BlockSpec(memory_space=pltpu.SMEM),
+            ),
             scratch_shapes=scratch,
             compiler_params=pltpu.CompilerParams(
                 collective_id=0, has_side_effects=True, vmem_limit_bytes=63 << 20

time: 29 us -> 28.5 us (0.983)
  Pallas kernels: 27.2 us -> 26.7 us
    pallas_call x1, Pallas kernels: 26.6 us -> 26.1 us  [local(): pl.pallas_call(functools.partial(kernel, nf, nm, blocks), out_shape=(jax....]
where the time goes in v5:
time: 28.5 us; the launch traced here: 28.4 us
  Pallas kernels  26.7 us (94%)
  between operations  1.41 us (5%)
    pallas_call x1, Pallas kernels, local(): pl.pallas_call(functools.partial(kernel, nf, nm, blocks), out_shape=(jax....  26.1 us
    pallas_call x1, Pallas kernels, local(): end(pressure, shift, aperture_rest)  0.63 us

profile of v5, /device:TPU:1, one launch (start us, length us, event | category | flops | bytes accessed | tf_op | source)
XLA Modules:
  0.0 28.4 jit_solution(14121434446784478129)
XLA Ops:
  0.6 0.0 copy-start
  0.6 0.0 copy-start.2
  0.7 0.0 copy-start.3
  0.7 0.0 copy-start.4
  0.7 0.0 copy-start.5
  0.7 26.1 %shard_map.106 = (f32[64,128]{1,0:T(8,128)S(1)}, f32[64,128]{1,0:T(8,128)S(1)}, f32[1,1]{1,0:T(1,128)}) custom-call(f32[64,128]{1,0:T(8,128)} %src_h.1, f32[64,128]{1,0:T(8,128)} %ap_h.1, f32[64,128]{1,0:T(8,128)} %st_h.1, f32[64,128]{1,0:T(8,128)} %ge_h.1, f32[64,128,128]{2,1,0:T(8,128)} %tiles_h.1, bf16[16,512,128]{2,1,0:T(8,128)(2,1)} %near_h.1, ...), custom_call_target="tpu_custom_call" | custom-call | tf_op jit(solution)/shard_map/pallas_call | solution.py:551
  27.4 0.0 copy-done
  27.5 0.0 copy-done.2
  27.5 0.0 copy-done.3
  27.5 0.0 copy-done.4
  27.5 0.0 copy-done.5
  27.5 0.9 %conditional.1 = ((f32[64,128]{1,0:T(8,128)}, f32[64,128]{1,0:T(8,128)})) conditional(s32[]{:T(128)} %bitcast.37, (f32[64,128]{1,0:T(8,128)S(1)}, f32[64,128]{1,0:T(8,128)S(1)}, f32[64,128]{1,0:T(8,128)S(1)}, f32[64,128,128]{2,1,0:T(8,128)}, f32[64,128]{1,0:T(8,128)S(1)}, /*index=5*/bf16[16,512,128]{2,1,0:T(8,128)(2,1)}, f32[8192,64]{0,1:T(8,128)}, ...), branch_computations={%region_0.0_spmd, %region_23.0_spmd} | conditional | flops 78751936 | bytes 39485336 | solution.py:578
  27.7 0.6 %branch_1_fun.1 = (f32[64,128]{1,0:T(8,128)}, f32[64,128]{1,0:T(8,128)}) custom-call(f32[64,128]{1,0:T(8,128)S(1)} %get-tuple-element.33.p_in, f32[64,128]{1,0:T(8,128)S(1)} %get-tuple-element.34.shift, f32[64,128]{1,0:T(8,128)S(1)} %get-tuple-element.35.rest), custom_call_target="tpu_custom_call" | custom-call | tf_op jit(solution)/shard_map/cond/branch_1_fun/pallas_call | solution.py:580
Async XLA Ops:
  0.6 26.8 %copy-start = (f32[64,128]{1,0:T(8,128)S(1)}, f32[64,128]{1,0:T(8,128)}, u32[]{:S(2)}) copy-start(f32[64,128]{1,0:T(8,128)} %ap_h.1) | copy-start | bytes 98308
  0.6 26.8 %copy-start.2 = (f32[64,128]{1,0:T(8,128)S(1)}, f32[64,128]{1,0:T(8,128)}, u32[]{:S(2)}) copy-start(f32[64,128]{1,0:T(8,128)} %src_h.1) | copy-start | bytes 98308
  0.7 26.8 %copy-start.3 = (f32[64,128]{1,0:T(8,128)S(1)}, f32[64,128]{1,0:T(8,128)}, u32[]{:S(2)}) copy-start(f32[64,128]{1,0:T(8,128)} %st_h.1) | copy-start | bytes 98308
  0.7 26.8 %copy-start.4 = (f32[64,128]{1,0:T(8,128)S(1)}, f32[64,128]{1,0:T(8,128)}, u32[]{:S(2)}) copy-start(f32[64,128]{1,0:T(8,128)} %ge_h.1) | copy-start | bytes 98308
  0.7 26.8 %copy-start.5 = (f32[64,64]{1,0:T(8,128)S(1)}, f32[64,64]{1,0:T(8,128)}, u32[]{:S(2)}) copy-start(f32[64,64]{1,0:T(8,128)} %core_h.1) | copy-start | bytes 49156

commit v6 on v5

--- a/solution.py
+++ b/solution.py
@@ -10,7 +10,7 @@
 BF16 = jnp.bfloat16
 MESH = pl.DeviceIdType.MESH
 NV = 5
-LEAST = 5e-5
+LEAST = 3e-3
 
 
 def split(x):
@@ -126,9 +126,9 @@
     src_h, ap_h, st_h, ge_h, tiles_h, near_h, bin_h, core_h, bout_h,
     p_h, a_h, f_h,
     ext, tiles, ghost, weights, near, bin_v, core, bout,
-    vec, img, diag, cnext, cprev, scale, p_v, a_v, f_v, far, rows,
+    vec, img, diag, cnext, cprev, scale, p_v, far, rows,
     m1, m2, m3, mz,
-    lsem, tsem, osem, xsem, bsem, zsem,
+    lsem, tsem, xsem, bsem, zsem,
 ):
     me = lax.axis_index("flow")
     owner = lax.axis_index("mech")
@@ -461,7 +461,7 @@
     p = coef[0] * vec[0, mid, :]
     for k in range(1, NV):
         p = p + coef[k] * vec[k, mid, :]
-    p_v[...] = p
+    p_v[0:blocks, :] = p
     f_h[0, 0] = least[0, 0]
     p_h[...] = p
 
@@ -481,7 +481,7 @@
                     c : c + 1, q * 128 : q * 128 + 128
                 ]
         piece = mz.at[owner, pl.ds(r * per * nm, per * nm)]
-        for d in range(1, nm):
+        for d in sorted(range(1, nm), key=lambda d: abs(2 * d - nm)):
             pltpu.make_async_remote_copy(
                 src_ref=piece,
                 dst_ref=piece,
@@ -540,11 +540,11 @@
             vm((rank, basis_in.shape[0]), F32),
             vm((NV, blocks + 32, width), F32), vm((NV,) + wide, F32),
             vm(wide, F32), vm(wide, F32), vm(wide, F32), vm(wide, F32),
-            vm(grid, F32), vm(grid, F32), vm((8, width), F32), vm(grid, F32), vm((32, width), F32),
-            vm(((nf + 1) * 8, width), F32), vm(((nf + 1) * 8, width), F32),
-            vm((nf * 8, width), F32), vm((nm,) + grid, F32),
+            vm((blocks + 8, width), F32), vm(grid, F32), vm((32, width), F32),
+            vm(((nf + 2) * 8, width), F32), vm(((nf + 2) * 8, width), F32),
+            vm(((nf + 1) * 8, width), F32), vm((nm,) + grid, F32),
             pltpu.SemaphoreType.DMA((8,)), pltpu.SemaphoreType.DMA((4,)),
-            pltpu.SemaphoreType.DMA((3,)), pltpu.SemaphoreType.DMA((4, 2)),
+            pltpu.SemaphoreType.DMA((4, 2)),
             pltpu.SemaphoreType.DMA((3, 2)), pltpu.SemaphoreType.DMA((4, 2)),
         ]
         anywhere = pl.BlockSpec(memory_space=pltpu.HBM)

time: 28.5 us -> 28.4 us (level)
  no operation moved by 1% of the time
where the time goes in v6:
time: 28.4 us; the launch traced here: 28.2 us
  Pallas kernels  26.6 us (94%)
  between operations  1.41 us (5%)
    pallas_call x1, Pallas kernels, local(): pl.pallas_call(functools.partial(kernel, nf, nm, blocks), out_shape=(jax....  25.9 us
    pallas_call x1, Pallas kernels, local(): end(pressure, shift, aperture_rest)  0.63 us

profile of v6, /device:TPU:1, one launch (start us, length us, event | category | flops | bytes accessed | tf_op | source)
XLA Modules:
  0.0 28.2 jit_solution(5617514849959620830)
XLA Ops:
  0.6 0.0 copy-start
  0.6 0.0 copy-start.2
  0.7 0.0 copy-start.3
  0.7 0.0 copy-start.4
  0.7 0.0 copy-start.5
  0.7 25.9 %shard_map.106 = (f32[64,128]{1,0:T(8,128)S(1)}, f32[64,128]{1,0:T(8,128)S(1)}, f32[1,1]{1,0:T(1,128)}) custom-call(f32[64,128]{1,0:T(8,128)} %src_h.1, f32[64,128]{1,0:T(8,128)} %ap_h.1, f32[64,128]{1,0:T(8,128)} %st_h.1, f32[64,128]{1,0:T(8,128)} %ge_h.1, f32[64,128,128]{2,1,0:T(8,128)} %tiles_h.1, bf16[16,512,128]{2,1,0:T(8,128)(2,1)} %near_h.1, ...), custom_call_target="tpu_custom_call" | custom-call | tf_op jit(solution)/shard_map/pallas_call | solution.py:551
  27.3 0.0 copy-done
  27.3 0.0 copy-done.2
  27.3 0.0 copy-done.3
  27.4 0.0 copy-done.4
  27.4 0.0 copy-done.5
  27.4 0.9 %conditional.1 = ((f32[64,128]{1,0:T(8,128)}, f32[64,128]{1,0:T(8,128)})) conditional(s32[]{:T(128)} %bitcast.37, (f32[64,128]{1,0:T(8,128)S(1)}, f32[64,128]{1,0:T(8,128)S(1)}, f32[64,128]{1,0:T(8,128)S(1)}, f32[64,128,128]{2,1,0:T(8,128)}, f32[64,128]{1,0:T(8,128)S(1)}, /*index=5*/bf16[16,512,128]{2,1,0:T(8,128)(2,1)}, f32[8192,64]{0,1:T(8,128)}, ...), branch_computations={%region_0.0_spmd, %region_23.0_spmd} | conditional | flops 78751936 | bytes 39485336 | solution.py:578
  27.6 0.6 %branch_1_fun.1 = (f32[64,128]{1,0:T(8,128)}, f32[64,128]{1,0:T(8,128)}) custom-call(f32[64,128]{1,0:T(8,128)S(1)} %get-tuple-element.33.p_in, f32[64,128]{1,0:T(8,128)S(1)} %get-tuple-element.34.shift, f32[64,128]{1,0:T(8,128)S(1)} %get-tuple-element.35.rest), custom_call_target="tpu_custom_call" | custom-call | tf_op jit(solution)/shard_map/cond/branch_1_fun/pallas_call | solution.py:580
Async XLA Ops:
  0.6 26.7 %copy-start = (f32[64,128]{1,0:T(8,128)S(1)}, f32[64,128]{1,0:T(8,128)}, u32[]{:S(2)}) copy-start(f32[64,128]{1,0:T(8,128)} %ap_h.1) | copy-start | bytes 98308
  0.6 26.7 %copy-start.2 = (f32[64,128]{1,0:T(8,128)S(1)}, f32[64,128]{1,0:T(8,128)}, u32[]{:S(2)}) copy-start(f32[64,128]{1,0:T(8,128)} %src_h.1) | copy-start | bytes 98308
  0.7 26.7 %copy-start.3 = (f32[64,128]{1,0:T(8,128)S(1)}, f32[64,128]{1,0:T(8,128)}, u32[]{:S(2)}) copy-start(f32[64,128]{1,0:T(8,128)} %st_h.1) | copy-start | bytes 98308
  0.7 26.7 %copy-start.4 = (f32[64,128]{1,0:T(8,128)S(1)}, f32[64,128]{1,0:T(8,128)}, u32[]{:S(2)}) copy-start(f32[64,128]{1,0:T(8,128)} %ge_h.1) | copy-start | bytes 98308
  0.7 26.7 %copy-start.5 = (f32[64,64]{1,0:T(8,128)S(1)}, f32[64,64]{1,0:T(8,128)}, u32[]{:S(2)}) copy-start(f32[64,64]{1,0:T(8,128)} %core_h.1) | copy-start | bytes 49156

commit v7 on v6

--- a/solution.py
+++ b/solution.py
@@ -470,8 +470,8 @@
     for q in range(nm):
         mine = jnp.where(owner == q, p_v[pl.ds(q, clusters, stride=nm), :], mine)
     mine = mine.astype(BF16)
-    per = clusters // 4
-    for r in range(4):
+    per = clusters // 2
+    for r in range(2):
         for c in range(r * per, (r + 1) * per):
             full_c = lax.dot_general(
                 mine, near[c], (((1,), (1,)), ((), ())), preferred_element_type=F32
@@ -511,7 +511,7 @@
         far[g : g + 1, :] = jnp.sum(
             bout[:, g * 128 : g * 128 + 128] * mixed, axis=0, keepdims=True
         )
-    for r in range(4):
+    for r in range(2):
         z_wait(r, 1)
     a_h[...] = jnp.sum(mz[...], axis=0) + far[...]
     for c in pending:
@@ -519,7 +519,7 @@
     gather_wait(m1, 0, 0, 3)
     gather_wait(m2, 1, 0, 3)
     gather_wait(m3, 2, 0, 3)
-    for r in range(4):
+    for r in range(2):
         z_wait(r, 0)
 
 

time: 28.4 us -> 28.3 us (level)
  no operation moved by 1% of the time
where the time goes in v7:
time: 28.3 us; the launch traced here: 28.2 us
  Pallas kernels  26.5 us (94%)
  between operations  1.41 us (5%)
    pallas_call x1, Pallas kernels, local(): pl.pallas_call(functools.partial(kernel, nf, nm, blocks), out_shape=(jax....  25.9 us
    pallas_call x1, Pallas kernels, local(): end(pressure, shift, aperture_rest)  0.63 us

profile of v7, /device:TPU:1, one launch (start us, length us, event | category | flops | bytes accessed | tf_op | source)
XLA Modules:
  0.0 28.2 jit_solution(7195590199996673782)
XLA Ops:
  0.6 0.0 copy-start
  0.6 0.0 copy-start.2
  0.7 0.0 copy-start.3
  0.7 0.0 copy-start.4
  0.7 0.0 copy-start.5
  0.7 25.9 %shard_map.106 = (f32[64,128]{1,0:T(8,128)S(1)}, f32[64,128]{1,0:T(8,128)S(1)}, f32[1,1]{1,0:T(1,128)}) custom-call(f32[64,128]{1,0:T(8,128)} %src_h.1, f32[64,128]{1,0:T(8,128)} %ap_h.1, f32[64,128]{1,0:T(8,128)} %st_h.1, f32[64,128]{1,0:T(8,128)} %ge_h.1, f32[64,128,128]{2,1,0:T(8,128)} %tiles_h.1, bf16[16,512,128]{2,1,0:T(8,128)(2,1)} %near_h.1, ...), custom_call_target="tpu_custom_call" | custom-call | tf_op jit(solution)/shard_map/pallas_call | solution.py:551
  27.2 0.0 copy-done
  27.3 0.0 copy-done.2
  27.3 0.0 copy-done.3
  27.3 0.0 copy-done.4
  27.3 0.0 copy-done.5
  27.3 0.9 %conditional.1 = ((f32[64,128]{1,0:T(8,128)}, f32[64,128]{1,0:T(8,128)})) conditional(s32[]{:T(128)} %bitcast.37, (f32[64,128]{1,0:T(8,128)S(1)}, f32[64,128]{1,0:T(8,128)S(1)}, f32[64,128]{1,0:T(8,128)S(1)}, f32[64,128,128]{2,1,0:T(8,128)}, f32[64,128]{1,0:T(8,128)S(1)}, /*index=5*/bf16[16,512,128]{2,1,0:T(8,128)(2,1)}, f32[8192,64]{0,1:T(8,128)}, ...), branch_computations={%region_0.0_spmd, %region_23.0_spmd} | conditional | flops 78751936 | bytes 39485336 | solution.py:578
  27.5 0.6 %branch_1_fun.1 = (f32[64,128]{1,0:T(8,128)}, f32[64,128]{1,0:T(8,128)}) custom-call(f32[64,128]{1,0:T(8,128)S(1)} %get-tuple-element.33.p_in, f32[64,128]{1,0:T(8,128)S(1)} %get-tuple-element.34.shift, f32[64,128]{1,0:T(8,128)S(1)} %get-tuple-element.35.rest), custom_call_target="tpu_custom_call" | custom-call | tf_op jit(solution)/shard_map/cond/branch_1_fun/pallas_call | solution.py:580
Async XLA Ops:
  0.6 26.6 %copy-start = (f32[64,128]{1,0:T(8,128)S(1)}, f32[64,128]{1,0:T(8,128)}, u32[]{:S(2)}) copy-start(f32[64,128]{1,0:T(8,128)} %ap_h.1) | copy-start | bytes 98308
  0.6 26.6 %copy-start.2 = (f32[64,128]{1,0:T(8,128)S(1)}, f32[64,128]{1,0:T(8,128)}, u32[]{:S(2)}) copy-start(f32[64,128]{1,0:T(8,128)} %src_h.1) | copy-start | bytes 98308
  0.7 26.6 %copy-start.3 = (f32[64,128]{1,0:T(8,128)S(1)}, f32[64,128]{1,0:T(8,128)}, u32[]{:S(2)}) copy-start(f32[64,128]{1,0:T(8,128)} %st_h.1) | copy-start | bytes 98308
  0.7 26.6 %copy-start.4 = (f32[64,128]{1,0:T(8,128)S(1)}, f32[64,128]{1,0:T(8,128)}, u32[]{:S(2)}) copy-start(f32[64,128]{1,0:T(8,128)} %ge_h.1) | copy-start | bytes 98308
  0.7 26.6 %copy-start.5 = (f32[64,64]{1,0:T(8,128)S(1)}, f32[64,64]{1,0:T(8,128)}, u32[]{:S(2)}) copy-start(f32[64,64]{1,0:T(8,128)} %core_h.1) | copy-start | bytes 49156
